TPU v7x, 32 devices: a whole 2x2x4 slice. The times are simulated.
32 devices in a mesh: dp: 16 (over z, y, core), tensor: 2 (over x).
Axes of the slice: x: 2, y: 2, z: 4, core: 2. Of those that a mesh axis runs over, the one named last changes fastest.
Arguments:
- tokens: bfloat16 [16384, 1024], P(('dp', 'tensor')), may hold values from -6 to 6
- cotangent: bfloat16 [16384, 1024], P(('dp', 'tensor')), may hold values from -6 to 6
- segment_ids: int32 [16384], P('dp'), may hold values from 0 to 4, as said below
- padding: int32 [16384], P('dp'), may hold values from 0 to 1, as said below
- shared_weights: float32 [2, 6297600], P('tensor', 'dp')
- first_moment: float32 [2, 16, 4, 393600], P('tensor', 'dp')
- second_moment: float32 [2, 16, 4, 393600], P('tensor', 'dp'), as said below
- outer_momentum: float32 [2, 6297600], P('tensor', 'dp'), may hold values from -0.04 to 0.04
Outputs:
- block_out: bfloat16 [16384, 1024], P(('dp', 'tensor'))
- input_grad: bfloat16 [16384, 1024], P(('dp', 'tensor'))
- group_grads: float32 [2, 16, 4, 393600], P('tensor', 'dp')
- group_first: float32 [2, 16, 4, 393600], P('tensor', 'dp')
- group_second: float32 [2, 16, 4, 393600], P('tensor', 'dp')
- group_weights: float32 [2, 16, 4, 393600], P('tensor', 'dp')
- mean_diff: float32 [2, 6297600], P('tensor', 'dp')
- new_momentum: float32 [2, 6297600], P('tensor', 'dp')
- new_weights: float32 [2, 6297600], P('tensor', 'dp')
Inputs may be any that keep to these rules, and one draw needn't show every extreme that they name: `segment_ids`: within each sequence of 1024 tokens the ids start at 0 and rise by one at each document boundary; a document has 60 to 800 tokens, except that a sequence's last one may be cut and its first one may be shorter, and each sequence holds a document of exactly 800 tokens. In each sequence the real tokens come first and at most 256 are padding; some sequence has no padding. `second_moment`: Positive.
All inputs are finite; a program needn't handle non-finite values.
Results may differ from a plain program's by a relative error of at most 0.018.
Values may be sent and summed in bfloat16 or wider, within the bound.
A program may use at most 256 MiB of HBM per device.

v0:
```python
import jax
import jax.numpy as jnp
from jax import lax
from jax.sharding import PartitionSpec as P

D = 1024
HEADS = 16
HD = 64
FF = 4096
SEQ_LEN = 1024
GROUPS = 4
STEP = 10


NORM_EPS = 1e-05
MASKED = -1000000000.0
BETA_ONE = 0.9
BETA_TWO = 0.999
ADAM_EPS = 1e-08
INNER_RATE = 0.02
DECAY = 0.01
OUTER_MU = 0.9
OUTER_RATE = 0.7
ROOT_HALF = 0.7071067811865476
INV_ROOT_TWO_PI = 0.3989422804014327


def from_partner(block, axis, stride):
    count = lax.axis_size(axis)
    route = []
    for low in range(count):
        high = low | 1 << stride
        if high != low and high < count:
            route += [(low, high), (high, low)]
    return lax.ppermute(block, axis, route)


def boundaries(tensor_size):
    local_width = D // tensor_size
    hidden = FF // tensor_size
    lengths = [
        3 * D * local_width,
        local_width * D,
        D * hidden,
        hidden * D,
        local_width,
        local_width,
        hidden,
        6 * local_width,
    ]
    points = [0]
    for amount in lengths:
        points.append(points[-1] + amount)
    return points


def layer_norm(values, norm_gain, norm_shift):
    average = jnp.mean(values, axis=-1, keepdims=True)
    centred = values - average
    variance = jnp.mean(centred * centred, axis=-1, keepdims=True)
    inv_dev = lax.rsqrt(variance + NORM_EPS)
    normed = centred * inv_dev
    return (normed * norm_gain + norm_shift, normed, inv_dev)


def norm_back(grad_normed, normed, inv_dev):
    first_part = jnp.mean(grad_normed, axis=-1, keepdims=True)
    second_part = jnp.mean(grad_normed * normed, axis=-1, keepdims=True)
    return inv_dev * (grad_normed - first_part - normed * second_part)


def gelu_slope(inner):
    return (
        0.5 * (1.0 + jax.scipy.special.erf(inner * ROOT_HALF))
        + inner * jnp.exp(-0.5 * inner * inner) * INV_ROOT_TWO_PI
    )


def row_contract(left_side, right_side):
    return lax.dot_general(
        left_side, right_side, (((0,), (0,)), ((), ())), preferred_element_type=jnp.float32
    )


def col_contract(left_side, right_side):
    return lax.dot_general(
        left_side, right_side, (((1,), (1,)), ((), ())), preferred_element_type=jnp.float32
    )


def halve_rounds(values, bit_list, first_axis, top_bit, dp_index, site_call):
    for bit_number in bit_list:
        axis_number = first_axis + top_bit - bit_number
        my_bit = dp_index >> bit_number & 1
        kept = lax.dynamic_index_in_dim(values, my_bit, axis_number, keepdims=True)
        outgoing = lax.dynamic_index_in_dim(values, 1 - my_bit, axis_number, keepdims=True)
        values = kept + site_call(outgoing, bit_number)
    return values


def local(
    tokens,
    cotangent,
    segment_ids,
    padding,
    shared_weights,
    first_moment,
    second_moment,
    outer_momentum,
):
    tensor_size = lax.axis_size("tensor")
    local_width = D // tensor_size
    hidden = FF // tensor_size
    local_heads = HEADS // tensor_size
    seq_rows = segment_ids.shape[0]
    seq_count = seq_rows // SEQ_LEN
    block_rows = min(512, SEQ_LEN)
    per_seq = SEQ_LEN // block_rows
    block_total = seq_count * per_seq
    score_scale = HD ** (-0.5)
    bf16 = jnp.bfloat16
    f32 = jnp.float32
    masters = lax.all_gather(shared_weights, "dp", axis=1, tiled=True)[0]
    points = boundaries(tensor_size)
    segments = [masters[points[number] : points[number + 1]] for number in range(8)]
    proj_weight = segments[0].reshape(3, D, local_width).astype(bf16)
    out_weight = segments[1].reshape(local_width, D).astype(bf16)
    in_weight = segments[2].reshape(D, hidden).astype(bf16)
    down_weight = segments[3].reshape(hidden, D).astype(bf16)
    query_bias = segments[4]
    value_bias = segments[5]
    inner_bias = segments[6]
    vectors = lax.all_gather(segments[7].reshape(6, local_width), "tensor", axis=1, tiled=True)
    inputs_all = lax.all_gather(tokens, "tensor", axis=0, tiled=True)
    projected = jnp.einsum("td,kde->kte", inputs_all, proj_weight, preferred_element_type=f32)
    query = (projected[0] + query_bias).astype(bf16)
    keys = projected[1].astype(bf16)
    values = (projected[2] + value_bias).astype(bf16)
    query_four = query.reshape(seq_count, SEQ_LEN, local_heads, HD)
    keys_four = keys.reshape(seq_count, SEQ_LEN, local_heads, HD)
    values_four = values.reshape(seq_count, SEQ_LEN, local_heads, HD)
    seg_two = segment_ids.reshape(seq_count, SEQ_LEN)
    live_two = padding.reshape(seq_count, SEQ_LEN)
    key_pos = jnp.arange(SEQ_LEN, dtype=jnp.int32)

    def block_scores(block_index):
        sequence = block_index // per_seq
        offset = block_index % per_seq * block_rows
        query_rows = lax.dynamic_index_in_dim(query_four, sequence, 0, keepdims=False)
        query_block = lax.dynamic_slice_in_dim(query_rows, offset, block_rows, 0)
        key_rows = lax.dynamic_index_in_dim(keys_four, sequence, 0, keepdims=False)
        seg_row = lax.dynamic_index_in_dim(seg_two, sequence, 0, keepdims=False)
        live_row = lax.dynamic_index_in_dim(live_two, sequence, 0, keepdims=False)
        seg_block = lax.dynamic_slice_in_dim(seg_row, offset, block_rows, 0)
        query_pos = offset + jnp.arange(block_rows, dtype=jnp.int32)
        allowed = (seg_block[:, None] == seg_row[None, :]) & (
            (live_row[None, :] == 1) | (query_pos[:, None] == key_pos[None, :])
        )
        raw_scores = (
            jnp.einsum("qhd,khd->hqk", query_block, key_rows, preferred_element_type=f32)
            * score_scale
        )
        return (
            jnp.where(allowed[None], raw_scores, MASKED),
            query_block,
            key_rows,
            sequence,
            offset,
        )

    def forward_block(block_index):
        scores, query_block, key_rows, sequence, offset = block_scores(block_index)
        value_rows = lax.dynamic_index_in_dim(values_four, sequence, 0, keepdims=False)
        highest = jnp.max(scores, axis=-1, keepdims=True)
        exponent = jnp.exp(scores - highest)
        summed = jnp.sum(exponent, axis=-1, keepdims=True)
        probabilities = (exponent / summed).astype(bf16)
        context = jnp.einsum("hqk,khd->qhd", probabilities, value_rows, preferred_element_type=f32)
        return (context, (highest + jnp.log(summed))[..., 0])

    context_blocks, log_totals = lax.map(forward_block, jnp.arange(block_total, dtype=jnp.int32))
    context_low = context_blocks.reshape(seq_rows, local_width).astype(bf16)
    attn_sum = lax.psum_scatter(
        jnp.dot(context_low, out_weight, preferred_element_type=f32).astype(jnp.bfloat16),
        "tensor",
        scatter_dimension=0,
        tiled=True,
    ).astype(jnp.float32)
    tokens_f = tokens.astype(f32)
    middle, normed_one, inv_one = layer_norm(
        tokens_f + (attn_sum + vectors[4]), vectors[0], vectors[1]
    )
    middle_all = lax.all_gather(middle.astype(bf16), "tensor", axis=0, tiled=True)
    inner = jnp.dot(middle_all, in_weight, preferred_element_type=f32) + inner_bias
    activated = jax.nn.gelu(inner, approximate=False).astype(bf16)
    ffn_sum = lax.psum_scatter(
        jnp.dot(activated, down_weight, preferred_element_type=f32).astype(jnp.bfloat16),
        "tensor",
        scatter_dimension=0,
        tiled=True,
    ).astype(jnp.float32)
    result, normed_two, inv_two = layer_norm(
        middle + (ffn_sum + vectors[5]), vectors[2], vectors[3]
    )
    block_out = result.astype(bf16)
    grad_out = cotangent.astype(f32)
    grad_gain_two = jnp.sum(grad_out * normed_two, axis=0)
    grad_shift_two = jnp.sum(grad_out, axis=0)
    grad_two = norm_back(grad_out * vectors[2], normed_two, inv_two)
    grad_down_bias = jnp.sum(grad_two, axis=0)
    back_all = lax.all_gather(grad_two.astype(bf16), "tensor", axis=0, tiled=True)
    grad_down_weight = row_contract(activated, back_all)
    grad_act = col_contract(back_all, down_weight)
    grad_inner = (grad_act * gelu_slope(inner)).astype(bf16)
    grad_inner_bias = jnp.sum(grad_inner.astype(f32), axis=0)
    grad_in_weight = row_contract(middle_all, grad_inner)
    grad_middle = grad_two + lax.psum_scatter(
        col_contract(grad_inner, in_weight).astype(jnp.bfloat16),
        "tensor",
        scatter_dimension=0,
        tiled=True,
    ).astype(jnp.float32)
    grad_gain_one = jnp.sum(grad_middle * normed_one, axis=0)
    grad_shift_one = jnp.sum(grad_middle, axis=0)
    grad_one = norm_back(grad_middle * vectors[0], normed_one, inv_one)
    grad_out_bias = jnp.sum(grad_one, axis=0)
    attn_back_all = lax.all_gather(grad_one.astype(bf16), "tensor", axis=0, tiled=True)
    grad_out_weight = row_contract(context_low, attn_back_all)
    grad_context = col_contract(attn_back_all, out_weight).astype(bf16)
    grad_context_four = grad_context.reshape(seq_count, SEQ_LEN, local_heads, HD)

    def backward_block(carry, block_index):
        grad_keys, grad_values = carry
        scores, query_block, key_rows, sequence, offset = block_scores(block_index)
        value_rows = lax.dynamic_index_in_dim(values_four, sequence, 0, keepdims=False)
        log_total = lax.dynamic_index_in_dim(log_totals, block_index, 0, keepdims=False)
        probabilities = jnp.exp(scores - log_total[..., None])
        prob_low = probabilities.astype(bf16)
        grad_rows = lax.dynamic_index_in_dim(grad_context_four, sequence, 0, keepdims=False)
        grad_block = lax.dynamic_slice_in_dim(grad_rows, offset, block_rows, 0)
        grad_probs = jnp.einsum("qhd,khd->hqk", grad_block, value_rows, preferred_element_type=f32)
        grad_scores = probabilities * (
            grad_probs - jnp.sum(grad_probs * probabilities, axis=-1, keepdims=True)
        )
        scores_low = grad_scores.astype(bf16)
        grad_query = (
            jnp.einsum("hqk,khd->qhd", scores_low, key_rows, preferred_element_type=f32)
            * score_scale
        )
        key_term = (
            jnp.einsum("hqk,qhd->khd", scores_low, query_block, preferred_element_type=f32)
            * score_scale
        )
        value_term = jnp.einsum("hqk,qhd->khd", prob_low, grad_block, preferred_element_type=f32)
        grad_keys = lax.dynamic_update_index_in_dim(
            grad_keys,
            lax.dynamic_index_in_dim(grad_keys, sequence, 0, keepdims=False) + key_term,
            sequence,
            0,
        )
        grad_values = lax.dynamic_update_index_in_dim(
            grad_values,
            lax.dynamic_index_in_dim(grad_values, sequence, 0, keepdims=False) + value_term,
            sequence,
            0,
        )
        return ((grad_keys, grad_values), grad_query)

    empty = jnp.zeros((seq_count, SEQ_LEN, local_heads, HD), f32)
    (grad_keys, grad_values), grad_queries = lax.scan(
        backward_block, (empty, empty), jnp.arange(block_total, dtype=jnp.int32)
    )
    grad_proj = jnp.stack(
        [
            grad_queries.reshape(seq_rows, local_width),
            grad_keys.reshape(seq_rows, local_width),
            grad_values.reshape(seq_rows, local_width),
        ]
    ).astype(bf16)
    grad_proj_weight = jnp.einsum("td,kte->kde", inputs_all, grad_proj, preferred_element_type=f32)
    grad_query_bias = jnp.sum(grad_proj[0].astype(f32), axis=0)
    grad_value_bias = jnp.sum(grad_proj[2].astype(f32), axis=0)
    input_part = jnp.einsum("kte,kde->td", grad_proj, proj_weight, preferred_element_type=f32)
    vector_part = jnp.stack(
        [
            grad_gain_one,
            grad_shift_one,
            grad_gain_two,
            grad_shift_two,
            grad_out_bias,
            grad_down_bias,
        ]
    )
    input_share, vector_grad = (
        lax.psum_scatter(
            input_part.astype(jnp.bfloat16), "tensor", scatter_dimension=0, tiled=True
        ).astype(jnp.float32),
        lax.psum_scatter(
            vector_part.astype(jnp.bfloat16), "tensor", scatter_dimension=1, tiled=True
        ).astype(jnp.float32),
    )
    input_grad = (grad_one + input_share).astype(bf16)
    flat_grad = jnp.concatenate(
        [
            grad_proj_weight.reshape(-1),
            grad_out_weight.reshape(-1),
            grad_in_weight.reshape(-1),
            grad_down_weight.reshape(-1),
            grad_query_bias,
            grad_value_bias,
            grad_inner_bias,
            vector_grad.reshape(-1),
        ]
    )
    dp_size = lax.axis_size("dp")
    per_group = dp_size // GROUPS
    inner_bits = per_group.bit_length() - 1
    all_bits = dp_size.bit_length() - 1
    dp_index = lax.axis_index("dp")
    slot_index = dp_index % per_group
    piece_len = shared_weights.shape[1]
    grid_view = flat_grad.reshape(GROUPS, per_group, piece_len)
    inner_list = list(range(inner_bits))
    outer_list = list(range(inner_bits, all_bits))
    inner_list = inner_list[::-1]
    outer_list = outer_list[::-1]
    summed_grid = grid_view
    for bit_number in inner_list:
        summed_grid = summed_grid + from_partner(
            summed_grid.astype(jnp.bfloat16), "dp", bit_number
        ).astype(summed_grid.dtype)
    grad_block = lax.dynamic_index_in_dim(summed_grid, slot_index, 1, keepdims=False)
    weights_block = lax.dynamic_index_in_dim(
        masters.reshape(GROUPS, per_group, piece_len), slot_index, 1, keepdims=False
    )
    matrix_count = (4 * D * D + 2 * D * FF) // tensor_size
    flat_index = (
        jnp.arange(GROUPS, dtype=jnp.int32)[:, None] * per_group + slot_index
    ) * piece_len + jnp.arange(piece_len, dtype=jnp.int32)[None, :]
    decay_mask = (flat_index < matrix_count).astype(f32)
    first_new = BETA_ONE * first_moment[0, 0] + (1 - BETA_ONE) * grad_block
    second_new = BETA_TWO * second_moment[0, 0] + (1 - BETA_TWO) * grad_block * grad_block
    first_hat = first_new / (1 - BETA_ONE**STEP)
    second_hat = second_new / (1 - BETA_TWO**STEP)
    group_weights = weights_block - INNER_RATE * (
        first_hat / (jnp.sqrt(second_hat) + ADAM_EPS) + DECAY * decay_mask * weights_block
    )
    difference = weights_block - group_weights

    def outer_swap(outgoing, bit_number):
        return from_partner(outgoing.astype(jnp.bfloat16), "dp", bit_number).astype(outgoing.dtype)

    outer_bits = all_bits - inner_bits
    diff_view = difference.reshape((2,) * outer_bits + (piece_len,))
    diff_sum = halve_rounds(diff_view, outer_list, 0, all_bits - 1, dp_index, outer_swap).reshape(
        piece_len
    )
    mean_diff = diff_sum / GROUPS
    new_momentum = OUTER_MU * outer_momentum[0] + mean_diff
    new_weights = shared_weights[0] - OUTER_RATE * (mean_diff + OUTER_MU * new_momentum)
    return (
        block_out,
        input_grad,
        grad_block[None, None],
        first_new[None, None],
        second_new[None, None],
        group_weights[None, None],
        mean_diff[None],
        new_momentum[None],
        new_weights[None],
    )


def solution(mesh):
    in_specs = (
        P(("dp", "tensor"), None),
        P(("dp", "tensor"), None),
        P("dp"),
        P("dp"),
        P("tensor", "dp"),
        P("tensor", "dp", None, None),
        P("tensor", "dp", None, None),
        P("tensor", "dp"),
    )
    out_specs = (
        P(("dp", "tensor"), None),
        P(("dp", "tensor"), None),
        P("tensor", "dp", None, None),
        P("tensor", "dp", None, None),
        P("tensor", "dp", None, None),
        P("tensor", "dp", None, None),
        P("tensor", "dp"),
        P("tensor", "dp"),
        P("tensor", "dp"),
    )
    return jax.shard_map(local, mesh=mesh, in_specs=in_specs, out_specs=out_specs, check_vma=False)
```

profile of v0, /device:TPU:8, one launch (start us, length us, event | category | flops | bytes accessed | tf_op | source)
XLA Modules:
  0.0 1800.6 jit_solution(1100648069684656320)
XLA Ops:
  8.7 130.8 %all-gather.6.cloned.1.call-done = f32[1,6297600]{1,0:T(1,128)} async-done(((f32[1,393600]{1,0:T(1,128)}), f32[1,6297600]{1,0:T(1,128)}) %all-gather.6.cloned.1.call-update) | async-done | bytes 25190416 | tf_op jit(solution)/shard_map/all_gather | solution.py:123
  140.1 265.3 %fusion.93 = (f32[6297600]{0:T(1024)}, bf16[1,6297600]{1,0:T(2,128)(2,1)}) fusion(f32[1,6297600]{1,0:T(1,128)} %all-gather.6.cloned.1.call-done, f32[]{:T(128)} %broadcast.514), kind=kLoop, calls=%fused_computation.195 | loop fusion | flops 6297600 | bytes 62976004 | tf_op jit(solution)/shard_map/all_gather | solution.py:123
  405.4 53.5 %slice_reduce_fusion.2 = bf16[1572864]{0:T(1024)(128)(2,1)S(1)} fusion(bf16[1,6297600]{1,0:T(2,128)(2,1)} %get-tuple-element.431), kind=kLoop, calls=%fused_computation.110 | loop fusion | bytes 6291456 | tf_op jit(solution)/shard_map/slice | solution.py:125
  459.0 3.9 convert_element_type.169
  462.9 6.0 convolution_bitcast_fusion.3
  472.2 22.8 %fusion.77 = bf16[524288]{0:T(1024)(128)(2,1)S(1)} fusion(f32[1,6297600]{1,0:T(1,128)} %all-gather.6.cloned.1.call-done), kind=kLoop, calls=%fused_computation.131 | loop fusion | bytes 2097152 | tf_op jit(solution)/shard_map/convert_element_type | solution.py:127
  499.9 34.2 %while.32 = (s32[]{:T(128)}, bf16[2,512,8,64]{1,3,2,0:T(8,128)(2,1)}, f32[2,8,512]{2,1,0:T(8,128)}, s32[2]{0:T(128)S(1)}, s32[1,1024]{1,0:T(1,128)S(1)}, /*index...) while((s32[]{:T(128)}, ...), condition=%wide.region_3.4_spmd.clone, body=%wide.region_0.3_spmd.clone.sunk | while | flops 1126168064 | bytes 64639360 | solution.py:181
  506.6 4.2 fusion.138
  510.9 5.4 fusion.139
  523.6 4.2 fusion.138
  527.8 5.4 fusion.139
  538.5 3.8 convolution_convert_fusion.2
  543.2 4.4 all_gather.20
  547.6 26.7 %reduce-scatter.6.cloned.1.call-done = bf16[512,1024]{1,0:T(8,128)(2,1)} async-done(((bf16[1024,1024]{1,0:T(8,128)(2,1)}), bf16[512,1024]{1,0:T(8,128)(2,1)}) %reduce-scatter.6.cloned.1.call-update) | async-done | bytes 1048592 | tf_op jit(solution)/shard_map/reduce_scatter | solution.py:183
  580.6 93.2 %slice_reduce_fusion = (bf16[2097152]{0:T(1024)(128)(2,1)}, bf16[2097152]{0:T(1024)(128)(2,1)}) fusion(bf16[1,6297600]{1,0:T(2,128)(2,1)} %get-tuple-element.431), kind=kLoop, calls=%fused_computation.76 | loop fusion | bytes 16777216 | tf_op jit(solution)/shard_map/slice | solution.py:125
  673.9 7.3 convert_element_type.182
  681.2 7.3 convert_element_type.180
  689.1 25.6 %fusion.47 = (bf16[1024,2048]{1,0:T(8,128)(2,1)S(1)}, f32[1024,2048]{1,0:T(8,128)}) fusion(f32[2048]{0:T(1024)S(1)} %bitcast.254, bf16[1024,1024]{1,0:T(8,128)(2,1)} %all-gather.10.cloned.1.call-done, bf16[1024,2048]{1,0:T(8,128)(2,1)} %convert_element_type.180), kind=kOutput, calls=%fused_computation.69 | convolution fusion | flops 4433379328 | bytes 18882560 | tf_op jit(solution)/shard_map/dot_general | solution.py:194
  716.7 5.6 convolution_convert_fusion.1
  722.4 31.9 %reduce-scatter.8.cloned.1.call-done = bf16[512,1024]{1,0:T(8,128)(2,1)} async-done(((bf16[1024,1024]{1,0:T(8,128)(2,1)}), bf16[512,1024]{1,0:T(8,128)(2,1)}) %reduce-scatter.8.cloned.1.call-update) | async-done | bytes 1048592 | tf_op jit(solution)/shard_map/reduce_scatter | solution.py:196
  760.9 33.2 %all-gather.12.cloned.1.call-done = bf16[1024,1024]{1,0:T(8,128)(2,1)} async-done(((bf16[512,1024]{1,0:T(8,128)(2,1)}), bf16[1024,1024]{1,0:T(8,128)(2,1)}) %all-gather.12.cloned.1.call-update) | async-done | bytes 2097168 | tf_op jit(solution)/shard_map/all_gather | solution.py:211
  794.1 11.9 convert_reduce_fusion
  808.0 5.7 convolution_convert_fusion
  814.0 31.7 %reduce-scatter.10.cloned.1.call-done = bf16[512,1024]{1,0:T(8,128)(2,1)} async-done(((bf16[1024,1024]{1,0:T(8,128)(2,1)}), bf16[512,1024]{1,0:T(8,128)(2,1)}) %reduce-scatter.10.cloned.1.call-update) | async-done | bytes 1048592 | tf_op jit(solution)/shard_map/reduce_scatter | solution.py:217
  849.1 3.5 fusion.89
  856.2 7.3 convolution_bitcast_fusion
  863.6 5.4 copy.41
  869.0 4.6 convolution_bitcast_fusion.1
  873.6 5.2 copy.40
  880.2 18.5 %all-gather.14.cloned.1.call-done = bf16[1024,1024]{1,0:T(8,128)(2,1)} async-done(((bf16[512,1024]{1,0:T(8,128)(2,1)}), bf16[1024,1024]{1,0:T(8,128)(2,1)}) %all-gather.14.cloned.1.call-update) | async-done | bytes 2097168 | tf_op jit(solution)/shard_map/all_gather | solution.py:227
  898.7 3.8 convolution_convert_fusion.3
  906.8 93.9 %while.33 = (s32[]{:T(128)}, f32[1,1024,8,64]{1,3,2,0:T(8,128)}, f32[1,1024,8,64]{1,3,2,0:T(8,128)}, bf16[2,512,8,64]{1,3,2,0:T(8,128)(2,1)}, s32[2]{0:T(128)S(1...) while((s32[]{:T(128)}, f32[1,1024,8,64]{1,3,2,0:T(8,128)}, ...), condition=%wide.region_17.18_spmd.clone, body=%wide.region_15.17_spmd.clone.sunk | while | flops 2726032896 | bytes 196186608 | solution.py:270
  912.3 5.9 subtract_exponential_fusion.3
  918.2 4.6 fusion.150
  922.8 10.3 multiply_reduce_fusion.7
  933.0 9.5 multiply_convert_fusion.2
  942.5 7.0 fusion.151
  959.1 5.9 subtract_exponential_fusion.3
  965.0 4.6 fusion.150
  969.6 10.3 multiply_reduce_fusion.7
  979.9 9.5 multiply_convert_fusion.2
  989.4 7.0 fusion.151
  1014.1 8.5 convolution_bitcast_fusion.2
  1022.6 6.6 copy.30
  1029.1 4.4 copy.38
  1040.6 4.3 constant_dynamic-update-slice_fusion.5
  1053.1 29.7 %reshape.539 = f32[4,4,393600]{2,1,0:T(4,128)} reshape(f32[6297600]{0:T(1024)} %constant_dynamic-update-slice_fusion) | data formatting | bytes 50380800 | tf_op jit(solution)/shard_map/reshape | solution.py:322
  1082.8 9.9 convert_element_type.199
  1094.3 271.0 %collective-permute-done = bf16[4,4,393600]{2,1,0:T(4,128)(2,1)} collective-permute-done((bf16[4,4,393600]{2,1,0:T(4,128)(2,1)S(1)}, bf16[4,4,393600]{2,1,0:T(4,128)(2,1)}, u32[]{:S(2)}, u32[]{:S(2)}) %collective-permute-start) | collective-permute-done | bytes 12595232 | tf_op jit(solution)/shard_map/ppermute | solution.py:35
  1365.2 29.6 %fusion.88 = (bf16[4,4,393600]{2,1,0:T(4,128)(2,1)}, f32[4,4,393600]{2,1,0:T(4,128)}) fusion(f32[4,4,393600]{2,1,0:T(4,128)} %reshape.539, bf16[4,4,393600]{2,1,0:T(4,128)(2,1)} %collective-permute-done), kind=kLoop, calls=%fused_computation.191 | loop fusion | flops 18892800 | bytes 75571200 | tf_op jit(solution)/shard_map/convert_element_type | solution.py:330
  1394.8 29.6 %reshape_squeeze.3 = f32[4,4,393600]{2,1,0:T(4,128)} reshape(f32[6297600]{0:T(1024)} %get-tuple-element.430) | data formatting | bytes 50380800 | tf_op jit(solution)/shard_map/reshape;squeeze | solution.py:334
  1424.5 72.1 %fusion.86 = (f32[4,393600]{1,0:T(4,128)}, f32[4,1,393600]{2,1,0:T(1,128)}) fusion(f32[]{:T(128)} %broadcast.514, f32[4,4,393600]{2,1,0:T(4,128)} %reshape_squeeze.3, s32[]{:T(128)S(6)} %select_n.102), kind=kLoop, calls=%fused_computation.190 | loop fusion | bytes 18892808 | tf_op jit(solution)/shard_map/jit(dynamic_index_in_dim)/dynamic_slice | solution.py:333
  1496.6 10.3 squeeze.88
  1506.9 77.4 %fusion.85 = (f32[4,393600]{1,0:T(4,128)}, f32[4,1,393600]{2,1,0:T(1,128)}) fusion(bf16[4,4,393600]{2,1,0:T(4,128)(2,1)} %collective-permute-done.1, s32[]{:T(128)S(6)} %select_n.102, f32[4,4,393600]{2,1,0:T(4,128)} %get-tuple-element.417), kind=kLoop, calls=%fused_computation.189 | loop fusion | flops 3148800 | bytes 22041604 | tf_op jit(solution)/shard_map/jit(dynamic_index_in_dim)/dynamic_slice | solution.py:332
  1584.2 10.2 squeeze.89
  1594.5 24.8 %bitcast_subtract_fusion = (f32[1,1,4,393600]{3,2,1,0:T(4,128)}, f32[1,1,4,393600]{3,2,1,0:T(4,128)}, f32[1,1,4,393600]{3,2,1,0:T(4,128)}, f32[1,1,4,393600]{3,2...) fusion(s32[4]{0:T(128)S(1)} %add_multiply_fusion.1, f32[4,1,393600]{2,1,0:T(1,128)} %get-tuple-element.411, ...), kind=kLoop, calls=%fused_computation.104 | loop fusion | flops 28339200 | bytes 62976016 | tf_op jit(solution)/shard_map/sub | solution.py:345
  1619.3 10.3 mul.388
  1629.6 10.3 mul.385
  1639.9 23.4 %subtract_subtract_fusion = f32[2,2,393600]{2,1,0:T(2,128)S(1)} fusion(f32[2,2,393600]{2,1,0:T(2,128)} %squeeze.88, f32[2,2,393600]{2,1,0:T(2,128)} %mul.385, f32[2,2,393600]{2,1,0:T(2,128)} %squeeze.89, f32[2,2,393600]{2,1,0:T(2,128)} %mul.388, s32[2,2]{1,0:T(2,128)S(1)} %add_multiply_fusion), kind=kLoop, calls=%fused_computation.64 | loop fusion | flops 26764800 | bytes 31488016 | tf_op jit(solution)/shard_map/sub | solution.py:348
  1670.7 6.6 bitcast_convert_fusion
  1677.3 61.8 %collective-permute-done.2 = bf16[1,2,393600]{2,1,0:T(2,128)(2,1)} collective-permute-done((bf16[1,2,393600]{2,1,0:T(2,128)(2,1)}, bf16[1,2,393600]{2,1,0:T(2,128)(2,1)}, u32[]{:S(2)}, u32[]{:S(2)}) %collective-permute-start.2) | collective-permute-done | bytes 1574432 | tf_op jit(solution)/shard_map/ppermute | solution.py:35
  1739.1 3.9 convert_add_fusion.1
  1751.3 32.6 %collective-permute-done.3 = bf16[1,1,393600]{2,1,0:T(2,128)(2,1)} collective-permute-done((bf16[1,1,393600]{2,1,0:T(2,128)(2,1)}, bf16[1,1,393600]{2,1,0:T(2,128)(2,1)}, u32[]{:S(2)}, u32[]{:S(2)}) %collective-permute-start.3) | collective-permute-done | bytes 787232 | tf_op jit(solution)/shard_map/ppermute | solution.py:35
  1784.0 9.4 multiply_subtract_fusion
  (220 shorter events, 114.6 us)
Async XLA Ops:
  7.2 132.4 %all-gather.6.cloned.1.call-start = ((), (), s32[]{:S(2)}) async-start(), calls=%async_computation.5 | async-start | bytes 26764800 | tf_op jit(solution)/shard_map/all_gather | solution.py:123
  7.9 454.9 %all-gather.8.cloned.1.call-start = ((), (), s32[]{:S(2)}) async-start(), calls=%async_computation.6 | async-start | bytes 3145728 | tf_op jit(solution)/shard_map/all_gather | solution.py:134
  8.7 565.7 %reduce-scatter.6.cloned.1.call-start = ((), (), s32[]{:S(2)}) async-start(), calls=%async_computation.7 | async-start | bytes 3145728 | tf_op jit(solution)/shard_map/reduce_scatter | solution.py:183
  472.2 27.7 %copy-start.26 = (s32[1024]{0:T(1024)S(1)}, s32[1024]{0:T(1024)}, u32[]{:S(2)}) copy-start(s32[1024]{0:T(1024)} %param.14) | copy-start | bytes 12292
  472.2 27.7 %copy-start.28 = (s32[1024]{0:T(1024)S(1)}, s32[1024]{0:T(1024)}, u32[]{:S(2)}) copy-start(s32[1024]{0:T(1024)} %param.15) | copy-start | bytes 12292
  506.6 4.3 copy-start.19
  516.3 1.0 copy-start.20
  523.5 4.3 copy-start.19
  533.2 1.0 copy-start.20
  534.2 3.1 copy-start.7
  534.2 8.2 copy-start.4
  534.2 8.2 copy-start.9
  537.3 37.1 %copy-start.6 = (bf16[512,1024]{1,0:T(8,128)(2,1)S(1)}, bf16[512,1024]{1,0:T(8,128)(2,1)}, u32[]{:S(2)}) copy-start(bf16[512,1024]{1,0:T(8,128)(2,1)} %param.12) | copy-start | bytes 3145732
  537.5 1.0 copy-start.22
  542.4 146.8 %all-gather.10.cloned.1.call-start = ((), (), s32[]{:S(2)}) async-start(), calls=%async_computation.8 | async-start | bytes 3145728 | tf_op jit(solution)/shard_map/all_gather | solution.py:193
  580.6 173.8 %reduce-scatter.8.cloned.1.call-start = ((), (), s32[]{:S(2)}) async-start(), calls=%async_computation.9 | async-start | bytes 3145728 | tf_op jit(solution)/shard_map/reduce_scatter | solution.py:196
  689.1 27.6 %copy-start.18 = (bf16[2048,1024]{1,0:T(8,128)(2,1)S(1)}, bf16[2048,1024]{1,0:T(8,128)(2,1)}, u32[]{:S(2)}) copy-start(bf16[2048,1024]{1,0:T(8,128)(2,1)} %convert_element_type.182) | copy-start | bytes 12582916
  714.7 2.0 copy-start.35
  716.7 37.7 %copy-start.8 = (bf16[512,1024]{1,0:T(8,128)(2,1)S(1)}, bf16[512,1024]{1,0:T(8,128)(2,1)}, u32[]{:S(2)}) copy-start(bf16[512,1024]{1,0:T(8,128)(2,1)} %reduce-scatter.6.cloned.1.call-done) | copy-start | bytes 3145732
  722.4 34.6 %copy-start.15 = (bf16[512,1024]{1,0:T(8,128)(2,1)S(1)}, bf16[512,1024]{1,0:T(8,128)(2,1)}, u32[]{:S(2)}) copy-start(bf16[512,1024]{1,0:T(8,128)(2,1)} %param.13) | copy-start | bytes 3145732
  722.4 71.7 %all-gather.12.cloned.1.call-start = ((), (), s32[]{:S(2)}) async-start(), calls=%async_computation.10 | async-start | bytes 3145728 | tf_op jit(solution)/shard_map/all_gather | solution.py:211
  760.8 84.9 %reduce-scatter.10.cloned.1.call-start = ((), (), s32[]{:S(2)}) async-start(), calls=%async_computation.11 | async-start | bytes 3145728 | tf_op jit(solution)/shard_map/reduce_scatter | solution.py:217
  794.1 13.9 copy-start.17
  806.0 2.0 copy-start.33
  813.7 65.1 %reduce-scatter.14.cloned.1.call-start = ((), (), s32[]{:S(2)}) async-start(), calls=%async_computation.14 | async-start | bytes 24576 | tf_op jit(solution)/shard_map/reduce_scatter | solution.py:298
  845.7 3.4 copy-start.12
  853.4 45.3 %all-gather.14.cloned.1.call-start = ((), (), s32[]{:S(2)}) async-start(), calls=%async_computation.12 | async-start | bytes 3145728 | tf_op jit(solution)/shard_map/all_gather | solution.py:227
  856.2 892.6 %reduce-scatter.12.cloned.1.call-start = ((), (), s32[]{:S(2)}) async-start(), calls=%async_computation.13 | async-start | bytes 3145728 | tf_op jit(solution)/shard_map/reduce_scatter | solution.py:295
  863.6 5.4 copy-start.32
  863.6 5.4 copy-start.34
  873.6 25.1 %copy-start.23 = (bf16[512,1024]{1,0:T(8,128)(2,1)S(1)}, bf16[512,1024]{1,0:T(8,128)(2,1)}, u32[]{:S(2)}) copy-start(bf16[512,1024]{1,0:T(8,128)(2,1)} %convert_element_type.176) | copy-start | bytes 3145732
  880.2 26.6 %copy-start.5 = (bf16[1,1024,8,64]{1,3,2,0:T(8,128)(2,1)S(1)}, bf16[1,1024,8,64]{1,3,2,0:T(8,128)(2,1)}, u32[]{:S(2)}) copy-start(bf16[1,1024,8,64]{1,3,2,0:T(8,128)(2,1)} %copy-done.4) | copy-start | bytes 3145732
  880.2 26.6 %copy-start.27 = (s32[1024]{0:T(1024)S(1)}, s32[1024]{0:T(1024)}, u32[]{:S(2)}) copy-start(s32[1024]{0:T(1024)} %param.14) | copy-start | bytes 12292
  880.2 26.6 %copy-start.29 = (s32[1024]{0:T(1024)S(1)}, s32[1024]{0:T(1024)}, u32[]{:S(2)}) copy-start(s32[1024]{0:T(1024)} %param.15) | copy-start | bytes 12292
  912.3 5.9 copy-start.10
  942.5 7.1 copy-start
  942.5 7.1 copy-start.1
  952.5 1.3 copy-start.2
  959.1 5.9 copy-start.10
  989.4 7.1 copy-start
  989.4 7.1 copy-start.1
  999.3 1.3 copy-start.2
  1004.3 6.3 copy-start.3
  1011.3 11.2 copy-start.24
  1014.1 8.5 copy-start.25
  1033.5 3.5 copy-start.16
  1033.6 5.8 slice-start.2
  1033.6 7.1 slice-start.3
  1037.0 7.9 slice-start
  1040.6 5.2 slice-start.1
  1045.9 6.1 copy-start.31
  1045.9 6.7 copy-start.30
  1092.7 272.5 %collective-permute-start = (bf16[4,4,393600]{2,1,0:T(4,128)(2,1)S(1)}, bf16[4,4,393600]{2,1,0:T(4,128)(2,1)}, u32[]{:S(2)}, u32[]{:S(2)}) collective-permute-start(bf16[4,4,393600]{2,1,0:T(4,128)(2,1)S(1)} %convert_element_type.199), channel_id=1, source_target_pairs={{0,4},{4,0},{2,6},{6,2},{8,12},{12,8},{10,14},{14,10},{16,20},{20,... | collective-permute-start | bytes 37785608 | tf_op jit(solution)/shard_map/ppermute | solution.py:35
  1394.8 112.1 %collective-permute-start.1 = (bf16[4,4,393600]{2,1,0:T(4,128)(2,1)}, bf16[4,4,393600]{2,1,0:T(4,128)(2,1)}, u32[]{:S(2)}, u32[]{:S(2)}) collective-permute-start(bf16[4,4,393600]{2,1,0:T(4,128)(2,1)} %get-tuple-element.416), channel_id=1, source_target_pairs={{0,2},{2,0},{4,6},{6,4},{8,10},{10,8},{12,14},{14,12},{16,18},{18,... | collective-permute-start | bytes 37785608 | tf_op jit(solution)/shard_map/ppermute | solution.py:35
  1639.9 30.8 %copy-start.21 = (bf16[3,1024,512]{2,1,0:T(8,128)(2,1)S(1)}, bf16[3,1024,512]{2,1,0:T(8,128)(2,1)}, u32[]{:S(2)}) copy-start(bf16[3,1024,512]{2,1,0:T(8,128)(2,1)} %convert_element_type.169) | copy-start | bytes 9437188
  1663.3 2.7 copy-start.11
  1668.3 70.8 %collective-permute-start.2 = (bf16[1,2,393600]{2,1,0:T(2,128)(2,1)}, bf16[1,2,393600]{2,1,0:T(2,128)(2,1)}, u32[]{:S(2)}, u32[]{:S(2)}) collective-permute-start(bf16[1,2,393600]{2,1,0:T(2,128)(2,1)} %dynamic-slice_convert_fusion.1), channel_id=1, source_target_pairs={{0,16},{16,0},{2,18},{18,2},{4,20},{20,4},{6,22},{22,6},{8,24},{24... | collective-permute-start | bytes 4723208 | tf_op jit(solution)/shard_map/ppermute | solution.py:35
  1677.3 71.5 %copy-start.13 = (f32[512,1024]{1,0:T(8,128)S(1)}, f32[512,1024]{1,0:T(8,128)}, u32[]{:S(2)}) copy-start(f32[512,1024]{1,0:T(8,128)} %get-tuple-element.419) | copy-start | bytes 6291460
  1743.0 1.7 copy-start.14
  1747.2 36.7 %collective-permute-start.3 = (bf16[1,1,393600]{2,1,0:T(2,128)(2,1)}, bf16[1,1,393600]{2,1,0:T(2,128)(2,1)}, u32[]{:S(2)}, u32[]{:S(2)}) collective-permute-start(bf16[1,1,393600]{2,1,0:T(2,128)(2,1)} %dynamic-slice_convert_fusion.2), channel_id=1, source_target_pairs={{0,8},{8,0},{2,10},{10,2},{4,12},{12,4},{6,14},{14,6},{16,24},{24,... | collective-permute-start | bytes 2361608 | tf_op jit(solution)/shard_map/ppermute | solution.py:35
Sparse Core Ops, SparseCore 0:
  9.6 129.8 all-gather.5
  141.1 33.0 all-gather.7
  542.5 31.8 reduce-scatter.5
  580.7 33.0 all-gather.9
  722.5 31.8 reduce-scatter.7
  760.9 33.1 all-gather.11
  813.9 31.8 reduce-scatter.9
  853.5 9.7 reduce-scatter.13
  865.5 33.1 all-gather.13
  1677.4 29.9 reduce-scatter.11
where the time goes:
time: 1810 us; the launch traced here: 1800 us
  waiting for transfers between devices  640 us (35%)
  other arithmetic  505 us (28%)
  local copies, waits for them, and re-layouts  448 us (25%)
  matrix products  171 us (9%)
    ppermute x4, waiting for transfers between devices, from_partner(): return lax.ppermute(block, axis, route)  365 us
    all_gather x1, other arithmetic, local(): masters = lax.all_gather(shared_weights, 'dp', axis=1, tiled=True)[0]  265 us
    slice x5, local copies, waits for them, and re-layouts, local(): masters[points[number]:points[number + 1]]  149 us
    all_gather x1, waiting for transfers between devices, local(): masters = lax.all_gather(shared_weights, 'dp', axis=1, tiled=True)[0]  131 us
    dynamic_slice x1, other arithmetic, local(): lax.dynamic_index_in_dim(summed_grid, slot_index, 1, keepdims=False)  77.4 us
    dynamic_slice x1, local copies, waits for them, and re-layouts, local(): lax.dynamic_index_in_dim(masters.reshape(GROUPS, per_group, piece_len), s...  72.1 us
    unnamed x80, local copies, waits for them, and re-layouts  45.4 us
    convert_element_type x2, other arithmetic, local(): summed_grid.astype(jnp.bfloat16)  39.5 us
  transfers between devices with their start and end apart: 14, of which 9 were waited for; matrix products, arithmetic and copies ran while one was open for 33% of the time, Pallas kernels for 0%

commit v1 on v0

--- a/solution.py
+++ b/solution.py
@@ -1,6 +1,12 @@
+import functools
+
 import jax
 import jax.numpy as jnp
+import numpy as np
 from jax import lax
+from jax.experimental import pallas as pl
+from jax.experimental.pallas import tpu as pltpu
+from jax.sharding import Mesh
 from jax.sharding import PartitionSpec as P
 
 D = 1024
@@ -98,7 +104,7 @@
     return values
 
 
-def local(
+def local_general(
     tokens,
     cotangent,
     segment_ids,
@@ -371,26 +377,923 @@
     )
 
 
+LANES = 128
+NT = (((1,), (1,)), ((), ()))
+NN = (((1,), (0,)), ((), ()))
+TN = (((0,), (0,)), ((), ()))
+VMEM_BYTES = 58 << 20
+f32 = jnp.float32
+bf16 = jnp.bfloat16
+
+
+def dot(left, right, dims):
+    return lax.dot_general(left, right, dims, preferred_element_type=f32)
+
+
+def params(**more):
+    return pltpu.CompilerParams(vmem_limit_bytes=VMEM_BYTES, **more)
+
+
+def round_up(number, step):
+    return -(-number // step) * step
+
+
+def attn_bwd_kernel(
+    q_ref, k_ref, v_ref, ctx_ref, dctx_ref, code_ref, seg_ref, lse_ref, dq_ref, dk_ref, dv_ref, *, rows_q
+):
+    n = q_ref.shape[0]
+    low = lax.broadcasted_iota(jnp.int32, (1, LANES), 1) < HD
+    zero = jnp.zeros((), bf16)
+    k = k_ref[...]
+    v = v_ref[...]
+    k_t = k.T
+    code = code_ref[...]
+    pick = (
+        lax.broadcasted_iota(jnp.int32, (8, LANES), 1) // HD
+        == lax.broadcasted_iota(jnp.int32, (8, LANES), 0)
+    ).astype(f32)
+    dks = [jnp.zeros((n, LANES), f32)] * 2
+    dvs = [jnp.zeros((n, LANES), f32)] * 2
+    scale = jnp.asarray(HD**-0.5, bf16)
+    for i in range(n // rows_q):
+        r = pl.ds(i * rows_q, rows_q)
+        q = q_ref[r, :] * scale
+        do = dctx_ref[r, :]
+        prod = do.astype(f32) * ctx_ref[r, :].astype(f32)
+        delta = lax.dot_general(
+            pick, prod, NT, precision=lax.Precision.HIGHEST, preferred_element_type=f32
+        )
+        keys = lax.broadcasted_iota(jnp.int32, (n, rows_q), 0)
+        qs = lax.broadcasted_iota(jnp.int32, (n, rows_q), 1) + i * rows_q
+        allowed = (code == seg_ref[:, r]) | (keys == qs)
+        dqs = []
+        for h in range(2):
+            qh = jnp.where(low, q, zero) if h == 0 else jnp.where(low, zero, q)
+            doh = jnp.where(low, do, zero) if h == 0 else jnp.where(low, zero, do)
+            s = jnp.where(allowed, dot(k, qh, NT), MASKED)
+            p = jnp.exp(s - lse_ref[0, h : h + 1, r])
+            dp = dot(v, doh, NT)
+            ds = (p * (dp - delta[h : h + 1])).astype(bf16)
+            dvs[h] = dvs[h] + dot(p.astype(bf16), do, NN)
+            dks[h] = dks[h] + dot(ds, q, NN)
+            dqs.append(dot(k_t[h * HD : (h + 1) * HD], ds, NN))
+        dq_ref[r, :] = (jnp.concatenate(dqs, axis=0).T * (HD**-0.5)).astype(bf16)
+    dk_ref[...] = jnp.where(low, dks[0], dks[1]).astype(bf16)
+    dv_ref[...] = jnp.where(low, dvs[0], dvs[1]).astype(bf16)
+
+
+def attn_bwd(q, k, v, ctx, dctx, code_col, seg_row, lse, rows_q=256):
+    n, w = q.shape
+    pairs = w // LANES
+    blk = pl.BlockSpec((n, LANES), lambda h: (0, h))
+    out = jax.ShapeDtypeStruct((n, w), bf16)
+    return pl.pallas_call(
+        functools.partial(attn_bwd_kernel, rows_q=rows_q),
+        grid=(pairs,),
+        in_specs=[blk] * 5
+        + [
+            pl.BlockSpec((n, 1), lambda h: (0, 0)),
+            pl.BlockSpec((1, n), lambda h: (0, 0)),
+            pl.BlockSpec((1, 2, n), lambda h: (h, 0, 0)),
+        ],
+        out_specs=[blk] * 3,
+        out_shape=[out] * 3,
+        cost_estimate=pl.CostEstimate(
+            flops=20 * n * n * w, bytes_accessed=16 * n * w, transcendentals=n * n * w // HD
+        ),
+        compiler_params=params(),
+        name="attn_bwd",
+    )(q, k, v, ctx, dctx, code_col, seg_row, lse)
+
+
+def matrix_table(tensor_size):
+    local_width = D // tensor_size
+    hidden = FF // tensor_size
+    table = []
+    offset = 0
+    for rows, columns in ((3 * D, local_width), (local_width, D), (D, hidden), (hidden, D)):
+        blocks = columns // LANES
+        table.append((offset, rows, blocks))
+        offset += rows * blocks
+    return table, offset
+
+
+def chunk_plan(table, first, end, tail_at, tail_rows):
+    segments = []
+    base = None
+    for number, (offset, rows, blocks) in enumerate(table):
+        low = max(first, offset)
+        high = min(end, offset + rows * blocks)
+        if low >= high:
+            continue
+        row_low = (low - offset) // blocks // 16 * 16
+        row_high = min(rows, round_up(-(-(high - offset) // blocks), 16))
+        if base is None:
+            base = offset + row_low * blocks
+        segments.append((number, row_low, row_high, blocks, offset + row_low * blocks - base))
+    size = max(at + (high - low) * blocks for _, low, high, blocks, at in segments)
+    if end > tail_at:
+        size = max(size, tail_at + tail_rows - base)
+    return segments, base, size
+
+
+def flatten_kernel(slot_ref, *refs, segments, skip, tail_at, tail_rows, per, piece_rows, padded):
+    count = len(segments)
+    keep, send, flat = refs[-3:]
+    for ref, (_, low, high, blocks, at) in zip(refs[:count], segments):
+        chunk = 16 if (high - low) % 64 else 64
+
+        @pl.loop(0, (high - low) // chunk)
+        def _(c, ref=ref, low=low, blocks=blocks, at=at, chunk=chunk):
+            rows = pl.ds(pl.multiple_of(low + c * chunk, 16), chunk)
+            for j in range(blocks):
+                to_rows = pl.ds(at + c * (chunk * blocks) + j, chunk, stride=blocks)
+                flat[to_rows, :] = ref[rows, j * LANES : (j + 1) * LANES].astype(f32)
+
+    if tail_at is not None:
+        flat[pl.ds(tail_at, tail_rows), :] = jnp.zeros((tail_rows, LANES), f32)
+    step = 128
+    full = piece_rows // step
+    rest = piece_rows - full * step
+    slot = slot_ref[0]
+    for j in range(per):
+        out = send if j % 2 else keep
+        start = skip + (slot ^ j) * piece_rows
+
+        @pl.loop(0, full)
+        def _(i, out=out, j=j, start=start):
+            rows = flat[pl.ds(start + i * step, step), :]
+            out[j // 2, pl.ds(pl.multiple_of(i * step, step), step), :] = rows.astype(bf16)
+
+        parts = [jnp.zeros((padded - piece_rows, LANES), f32)]
+        if rest:
+            parts = [flat[pl.ds(start + full * step, rest), :]] + parts
+        out[j // 2, full * step : padded, :] = jnp.concatenate(parts, axis=0).astype(bf16)
+
+
+def flatten(b, slot, matrices, table, tail_at, tail_rows, per, piece_rows, padded):
+    first = b * per * piece_rows
+    end = first + per * piece_rows
+    segments, base, size = chunk_plan(table, first, end, tail_at, tail_rows)
+    operands = [matrices[segment[0]] for segment in segments]
+    whole = pl.BlockSpec(memory_space=pltpu.VMEM)
+    shape = jax.ShapeDtypeStruct((per // 2, padded, LANES), bf16)
+    return pl.pallas_call(
+        functools.partial(
+            flatten_kernel,
+            segments=segments,
+            skip=first - base,
+            tail_at=tail_at - base if end > tail_at else None,
+            tail_rows=tail_rows,
+            per=per,
+            piece_rows=piece_rows,
+            padded=padded,
+        ),
+        in_specs=[pl.BlockSpec(memory_space=pltpu.SMEM)] + [whole] * len(operands),
+        out_specs=[whole, whole],
+        out_shape=[shape, shape],
+        scratch_shapes=[pltpu.VMEM((size + 8, LANES), f32)],
+        cost_estimate=pl.CostEstimate(
+            flops=per * piece_rows * LANES,
+            bytes_accessed=6 * per * piece_rows * LANES,
+            transcendentals=0,
+        ),
+        compiler_params=params(),
+        name=f"flatten_{b}",
+    )(slot, *operands)
+
+
+def row_parts(rows, count):
+    size = rows // count // 16 * 16
+    starts = [size * i for i in range(count)] + [rows]
+    return [(low, high - low) for low, high in zip(starts[:-1], starts[1:])]
+
+
+def in_steps(start, rows, step, body):
+    @pl.loop(0, rows // step)
+    def _(i):
+        body(pl.multiple_of(start + i * step, 16), step)
+
+    if rows % step:
+        body(start + rows // step * step, rows % step)
+
+
+def adamw_kernel(slot_ref, keep, near, far, w_ref, m_hbm, v_hbm, *refs, b, piece_rows, matrix_row, parts):
+    go, mo, vo, wo, d_ref, m_in, v_in, g_out, m_out, v_out, w_out, sems = refs[-12:]
+    loads = []
+    for n, (at, rows) in enumerate(parts):
+        r = pl.ds(at, rows)
+        pair = (
+            pltpu.make_async_copy(m_hbm.at[r, b, :], m_in.at[r], sems.at[0, n]),
+            pltpu.make_async_copy(v_hbm.at[r, b, :], v_in.at[r], sems.at[1, n]),
+        )
+        for copy in pair:
+            copy.start()
+        loads.append(pair)
+    stores = []
+
+    def update(at, rows):
+        r = pl.ds(at, rows)
+        g = keep[0, r, :].astype(f32) + near[0, r, :].astype(f32) + far[r, :].astype(f32)
+        w = w_ref[0, r, :].astype(f32)
+        m_new = BETA_ONE * m_in[r, :] + (1 - BETA_ONE) * g
+        v_new = BETA_TWO * v_in[r, :] + (1 - BETA_TWO) * g * g
+        root = jnp.sqrt(v_new * (1 / (1 - BETA_TWO**STEP))) + ADAM_EPS
+        decay = INNER_RATE * DECAY
+        if matrix_row is not None:
+            here = lax.broadcasted_iota(jnp.int32, (rows, LANES), 0) + at
+            decay = jnp.where(here < matrix_row[0] - slot_ref[0] * piece_rows, decay, 0.0)
+        d = (INNER_RATE / (1 - BETA_ONE**STEP)) * m_new / root + decay * w
+        g_out[r, :] = g
+        m_out[r, :] = m_new
+        v_out[r, :] = v_new
+        w_out[r, :] = w - d
+        d_ref[r, :] = d.astype(bf16)
+
+    for n, (at, rows) in enumerate(parts):
+        for copy in loads[n]:
+            copy.wait()
+        in_steps(at, rows, 64, update)
+        r = pl.ds(at, rows)
+        for k, (src, dst) in enumerate(((g_out, go), (m_out, mo), (v_out, vo), (w_out, wo))):
+            copy = pltpu.make_async_copy(src.at[r], dst.at[r, b, :], sems.at[2 + k, n])
+            copy.start()
+            stores.append(copy)
+    for copy in stores:
+        copy.wait()
+
+
+def adamw(b, slot, keep, near, far, pieces, first, second, held, per, matrix_rows):
+    piece_rows = first.shape[0]
+    padded = far.shape[0]
+    hbm = pl.BlockSpec(memory_space=pl.ANY)
+    shape = jax.ShapeDtypeStruct(first.shape, f32)
+    state = pltpu.VMEM((piece_rows, LANES), f32)
+    parts = row_parts(piece_rows, 3)
+    matrix_row = None
+    if (b + 1) * per * piece_rows > matrix_rows:
+        matrix_row = (matrix_rows - b * per * piece_rows,)
+    return pl.pallas_call(
+        functools.partial(
+            adamw_kernel, b=b, piece_rows=piece_rows, matrix_row=matrix_row, parts=parts
+        ),
+        grid_spec=pltpu.PrefetchScalarGridSpec(
+            num_scalar_prefetch=1,
+            grid=(1,),
+            in_specs=[
+                pl.BlockSpec((1, padded, LANES), lambda i, s: (0, 0, 0)),
+                pl.BlockSpec((1, padded, LANES), lambda i, s: (0, 0, 0)),
+                pl.BlockSpec((padded, LANES), lambda i, s: (0, 0)),
+                pl.BlockSpec((1, padded, LANES), lambda i, s: (b, 0, 0)),
+                hbm,
+                hbm,
+            ]
+            + [hbm] * len(held),
+            out_specs=[hbm] * 4 + [pl.BlockSpec((padded, LANES), lambda i, s: (0, 0))],
+            scratch_shapes=[state] * 6 + [pltpu.SemaphoreType.DMA((6, len(parts)))],
+        ),
+        out_shape=[shape] * 4 + [jax.ShapeDtypeStruct((padded, LANES), bf16)],
+        input_output_aliases={7 + k: k for k in range(len(held))},
+        cost_estimate=pl.CostEstimate(
+            flops=30 * piece_rows * LANES,
+            bytes_accessed=30 * piece_rows * LANES,
+            transcendentals=2 * piece_rows * LANES,
+        ),
+        compiler_params=params(),
+        name=f"adamw_{b}",
+    )(slot, keep, near, far, pieces, first, second, *held)
+
+
+def outer_kernel(d0, d1, d2, d3, w_hbm, o_hbm, mean_out, mom_out, new_out, w_in, o_in, mean, mom, new, sems, *, parts):
+    loads = []
+    for n, (at, rows) in enumerate(parts):
+        r = pl.ds(at, rows)
+        pair = (
+            pltpu.make_async_copy(w_hbm.at[r, 0, :], w_in.at[r], sems.at[0, n]),
+            pltpu.make_async_copy(o_hbm.at[r, 0, :], o_in.at[r], sems.at[1, n]),
+        )
+        for copy in pair:
+            copy.start()
+        loads.append(pair)
+    stores = []
+
+    def update(at, rows):
+        r = pl.ds(at, rows)
+        total = (d0[r, :].astype(f32) + d1[r, :].astype(f32)) + (
+            d2[r, :].astype(f32) + d3[r, :].astype(f32)
+        )
+        average = total / GROUPS
+        momentum = OUTER_MU * o_in[r, :] + average
+        mean[r, :] = average
+        mom[r, :] = momentum
+        new[r, :] = w_in[r, :] - OUTER_RATE * (average + OUTER_MU * momentum)
+
+    for n, (at, rows) in enumerate(parts):
+        for copy in loads[n]:
+            copy.wait()
+        in_steps(at, rows, 64, update)
+        r = pl.ds(at, rows)
+        for k, (src, dst) in enumerate(((mean, mean_out), (mom, mom_out), (new, new_out))):
+            copy = pltpu.make_async_copy(src.at[r], dst.at[r, 0, :], sems.at[2 + k, n])
+            copy.start()
+            stores.append(copy)
+    for copy in stores:
+        copy.wait()
+
+
+def outer(diffs, own_rows, momentum_rows):
+    piece_rows = own_rows.shape[0]
+    hbm = pl.BlockSpec(memory_space=pl.ANY)
+    whole = pl.BlockSpec(memory_space=pltpu.VMEM)
+    parts = row_parts(piece_rows, 3)
+    return pl.pallas_call(
+        functools.partial(outer_kernel, parts=parts),
+        in_specs=[whole] * 4 + [hbm] * 2,
+        out_specs=[hbm] * 3,
+        out_shape=[jax.ShapeDtypeStruct(own_rows.shape, f32)] * 3,
+        scratch_shapes=[pltpu.VMEM((piece_rows, LANES), f32)] * 5
+        + [pltpu.SemaphoreType.DMA((5, len(parts)))],
+        compiler_params=params(),
+        name="outer_step",
+    )(*diffs, own_rows, momentum_rows)
+
+
+def attend_block(q, k, v_ones, code, seg_col, offset):
+    rows_q, n = q.shape[0], k.shape[0]
+    low = lax.broadcasted_iota(jnp.int32, (1, LANES), 1) < HD
+    zero = jnp.zeros((), bf16)
+    q = q * jnp.asarray(HD**-0.5, bf16)
+    rows = lax.broadcasted_iota(jnp.int32, (rows_q, n), 0) + offset
+    cols = lax.broadcasted_iota(jnp.int32, (rows_q, n), 1)
+    allowed = (seg_col == code) | (rows == cols)
+    outs = []
+    tops = []
+    for h in range(2):
+        qh = jnp.where(low, q, zero) if h == 0 else jnp.where(low, zero, q)
+        s = jnp.where(allowed, dot(qh, k, NT), MASKED)
+        top = jnp.max(s, axis=1, keepdims=True)
+        p = jnp.exp(s - top).astype(bf16)
+        outs.append(dot(p, v_ones[h], NN))
+        tops.append(top)
+    num = jnp.where(low, outs[0], outs[1])
+    den = pltpu.roll(jnp.where(low, outs[1], outs[0]), HD, 1)
+    lse = (jnp.where(low, tops[0], tops[1]) + jnp.log(den)).T
+    return (num / den).astype(bf16), lse[0:1], lse[HD : HD + 1]
+
+
+def bring_rows(buf, flat, margin, offset, count, piece_rows):
+    for p in range(offset // piece_rows, -(-(offset + count) // piece_rows)):
+        low = max(offset - p * piece_rows, 0) // 16 * 16
+        high = min(round_up(min(offset + count - p * piece_rows, piece_rows), 16), buf.shape[1])
+        to = margin + p * piece_rows + low - offset
+        step = 128
+        full = (high - low) // step
+
+        @pl.loop(0, full)
+        def _(i, p=p, low=low, to=to):
+            rows = buf[p, pl.ds(pl.multiple_of(low + i * step, 16), step), :]
+            flat[pl.ds(to + i * step, step), :] = rows.astype(f32)
+
+        rest = (high - low) % step
+        if rest:
+            flat[pl.ds(to + full * step, rest), :] = buf[p, low + full * step : high, :].astype(f32)
+
+
+def emit_matrix(flat, out, margin, rows, blocks):
+    chunk = 64
+
+    @pl.loop(0, rows // chunk)
+    def _(c):
+        at = pl.ds(pl.multiple_of(c * chunk, chunk), chunk)
+        for j in range(blocks):
+            from_rows = pl.ds(margin + c * (chunk * blocks) + j, chunk, stride=blocks)
+            out[at, j * LANES : (j + 1) * LANES] = flat[from_rows, :].astype(bf16)
+
+
+def start_kernel(
+    own_hbm, tokens_hbm, code_ref, seg_ref,
+    proj_out, outw_out, inw_out, down_out, pieces_out, tail_out, x_out, q_ref, k_ref, v_ref, ctx_ref, lse_ref,
+    rows32, buf, xbuf, flat, proj_s, outw_s, inw_s, down_s,
+    zdown, zup, zrecv, ysend, yrecv, csend, crecv, xsem, local_sems,
+    *, piece_rows, tail_rows, table, cuts, rows_q
+):
+    z = lax.axis_index("group")
+    slot = lax.axis_index("slot")
+    me = lax.axis_index("tensor")
+    depth = GROUPS
+    padded = buf.shape[1]
+    half = tokens_hbm.shape[0]
+    n = 2 * half
+    mesh_id = pl.DeviceIdType.MESH
+
+    load = pltpu.make_async_copy(own_hbm.at[:, 0, :], rows32, local_sems.at[0])
+    load.start()
+    x_load = pltpu.make_async_copy(tokens_hbm, xbuf.at[pl.ds(0, half)], local_sems.at[1])
+    x_load.start()
+
+    barrier = pltpu.get_barrier_semaphore()
+    for where in ({"slot": slot ^ 1}, {"slot": slot ^ 2}, {"tensor": 1 - me}):
+        pl.semaphore_signal(barrier, inc=1, device_id=where, device_id_type=mesh_id)
+
+    @pl.when(z > 0)
+    def _():
+        pl.semaphore_signal(barrier, inc=1, device_id={"group": z - 1}, device_id_type=mesh_id)
+
+    @pl.when(z < depth - 1)
+    def _():
+        pl.semaphore_signal(barrier, inc=1, device_id={"group": z + 1}, device_id_type=mesh_id)
+
+    pl.semaphore_wait(barrier, 3 + jnp.where(z > 0, 1, 0) + jnp.where(z < depth - 1, 1, 0))
+
+    load.wait()
+    own = z * 4 + slot
+    step = 128
+    full = piece_rows // step
+
+    @pl.loop(0, full)
+    def _(i):
+        r = pl.ds(pl.multiple_of(i * step, step), step)
+        buf[own, r, :] = rows32[r, :].astype(bf16)
+
+    tail = rows32[piece_rows - tail_rows :, :]
+    left = tail - tail.astype(bf16).astype(f32)
+    zeros = jnp.zeros((padded - piece_rows - tail_rows, LANES), f32)
+    buf[own, full * step :, :] = jnp.concatenate([rows32[full * step :, :], left, zeros], axis=0).astype(bf16)
+
+    def copy_of(piece, h, send, recv, where):
+        part = buf.at[piece, pl.ds(*cuts[h])]
+        return pltpu.make_async_remote_copy(
+            src_ref=part, dst_ref=part, send_sem=send, recv_sem=recv, device_id=where, device_id_type=mesh_id
+        )
+
+    def down(b, h):
+        return copy_of(b * 4 + slot, h, zdown.at[b, h], zrecv.at[b, h], {"group": z + 1})
+
+    def up(b, h):
+        return copy_of(b * 4 + slot, h, zup.at[b, h], zrecv.at[b, h], {"group": z - 1})
+
+    def side(b, h):
+        return copy_of(b * 4 + slot, h, ysend.at[b, h], yrecv.at[b, h], {"slot": slot ^ 2})
+
+    def side_in(b, h):
+        return copy_of(b * 4 + (slot ^ 2), h, ysend.at[b, h], yrecv.at[b, h], {"slot": slot ^ 2})
+
+    def twin(b, h, k):
+        return copy_of(
+            b * 4 + (slot ^ (2 * k)), h, csend.at[2 * b + k, h], crecv.at[2 * b + k, h], {"slot": slot ^ 1}
+        )
+
+    def twin_in(b, h, k):
+        return copy_of(
+            b * 4 + (slot ^ 1 ^ (2 * k)), h, csend.at[2 * b + k, h], crecv.at[2 * b + k, h], {"slot": slot ^ 1}
+        )
+
+    parts = range(len(cuts))
+    tail_part = len(cuts) - 1
+    order = [tail_part] + list(range(tail_part))
+    last = depth - 1
+    ranked = (
+        z,
+        jnp.where(z == 0, 1, 0),
+        jnp.where(z == 2, 3, 2),
+        jnp.where(z < 2, 3, 1),
+    )
+    middle = (z == 1) | (z == 2)
+
+    def pass_on(b, h):
+        up(b, h).wait_recv()
+
+        @pl.when((b < z) & (z < last))
+        def _():
+            down(b, h).start()
+
+        @pl.when((b > z) & (z > 0))
+        def _():
+            up(b, h).start()
+
+        side(b, h).start()
+        twin(b, h, 0).start()
+
+    def serve_z(b, h, when=None):
+        if h == tail_part:
+            when = (b != last) if when is None else when & (b != last)
+        if when is None:
+            pass_on(b, h)
+        else:
+            pl.when(when)(functools.partial(pass_on, b, h))
+
+    def serve_y(rank, h):
+        b = ranked[rank]
+
+        def go():
+            side_in(b, h).wait_recv()
+            twin(b, h, 1).start()
+
+        if h == tail_part:
+            pl.when(b != last)(go)
+        else:
+            go()
+
+    early = order[:3]
+    for h in order:
+
+        @pl.when(z > 0)
+        def _(h=h):
+            up(z, h).start()
+
+        @pl.when(z == 0)
+        def _(h=h):
+            down(z, h).start()
+
+        if h in early:
+            side(z, h).start()
+        twin(z, h, 0).start()
+
+    x_load.wait()
+    x_copy = pltpu.make_async_remote_copy(
+        src_ref=xbuf.at[pl.ds(0, half)],
+        dst_ref=xbuf.at[pl.ds(half, half)],
+        send_sem=xsem.at[0],
+        recv_sem=xsem.at[1],
+        device_id={"tensor": 1 - me},
+        device_id_type=mesh_id,
+    )
+    x_copy.start()
+
+    pl.when(z != last)(functools.partial(pass_on, last, tail_part))
+    for h in order:
+        serve_z(ranked[1], h)
+    for h in order:
+
+        @pl.when((z > 0) & (z < last))
+        def _(h=h):
+            down(z, h).start()
+
+        if h not in early:
+            side(z, h).start()
+    for h in order:
+        serve_z(ranked[2], h, middle)
+    side_in(last, tail_part).wait_recv()
+    twin(last, tail_part, 1).start()
+    for h in early:
+        serve_y(0, h)
+    for h in order:
+        serve_y(1, h)
+    for h in order:
+        if h not in early:
+            serve_y(0, h)
+    for k in range(2):
+        twin_in(last, tail_part, k).wait_recv()
+        for rank in range(2):
+            b = ranked[rank]
+            for h in parts:
+                if h == tail_part:
+                    pl.when(b != last)(lambda b=b, h=h, k=k: twin_in(b, h, k).wait_recv())
+                else:
+                    twin_in(b, h, k).wait_recv()
+
+    at = (piece_rows - tail_rows) // 16 * 16
+    shift = piece_rows - tail_rows - at
+    ends = buf[4 * depth - 1, at:, :].astype(f32)
+    vectors = ends[shift : shift + tail_rows] + ends[shift + tail_rows : shift + 2 * tail_rows]
+    tail_out[...] = vectors
+
+    margin = 16
+    (offset, rows, blocks) = table[0]
+    bring_rows(buf, flat, margin, offset, rows * blocks, piece_rows)
+    emit_matrix(flat, proj_s, margin, rows, blocks)
+    out_copies = [pltpu.make_async_copy(proj_s, proj_out, local_sems.at[2])]
+    out_copies[0].start()
+    x_copy.wait()
+    out_copies.append(pltpu.make_async_copy(xbuf, x_out, local_sems.at[3]))
+    out_copies[1].start()
+    query_bias = jnp.concatenate([vectors[j : j + 1] for j in range(blocks)], axis=1)
+    value_bias = jnp.concatenate([vectors[blocks + j : blocks + j + 1] for j in range(blocks)], axis=1)
+    depth_in = rows // 3
+    for m, (ref, bias) in enumerate(((q_ref, query_bias), (k_ref, None), (v_ref, value_bias))):
+
+        @pl.loop(0, n // 256)
+        def _(i, m=m, ref=ref, bias=bias):
+            r = pl.ds(pl.multiple_of(i * 256, 256), 256)
+            acc = dot(xbuf[r, :], proj_s[m * depth_in : (m + 1) * depth_in, :], NN)
+            if bias is not None:
+                acc = acc + bias
+            ref[r, :] = acc.astype(bf16)
+
+        for h in order[2 * m : 2 * m + 2]:
+            serve_z(jnp.where(middle, ranked[3], ranked[2]), h)
+
+    edge = jnp.logical_not(middle)
+    todo = [functools.partial(serve_z, ranked[3], h, edge) for h in order]
+    late = [functools.partial(serve_y, 2, h) for h in order]
+    todo = [act for both_acts in zip(late, todo) for act in both_acts]
+    todo += [functools.partial(serve_y, 3, h) for h in order]
+    low = lax.broadcasted_iota(jnp.int32, (1, LANES), 1) < HD
+    one = jnp.ones((), bf16)
+    code = code_ref[...]
+    for pair in range(blocks):
+        c = slice(pair * LANES, (pair + 1) * LANES)
+        k = k_ref[:, c]
+        v = v_ref[:, c]
+        v_ones = (jnp.where(low, v, one), jnp.where(low, one, v))
+        for i in range(n // rows_q):
+            r = slice(i * rows_q, (i + 1) * rows_q)
+            ctx, lse_0, lse_1 = attend_block(q_ref[r, c], k, v_ones, code, seg_ref[r, :], i * rows_q)
+            ctx_ref[r, c] = ctx
+            lse_ref[pair, 0:1, r] = lse_0
+            lse_ref[pair, 1:2, r] = lse_1
+            for _ in range(1):
+                if todo:
+                    todo.pop(0)()
+    for act in todo:
+        act()
+    for rank in range(2, 4):
+        b = ranked[rank]
+        for h in parts:
+            for k in range(2):
+                if h == tail_part:
+                    pl.when(b != last)(lambda b=b, h=h, k=k: twin_in(b, h, k).wait_recv())
+                else:
+                    twin_in(b, h, k).wait_recv()
+
+    for b in range(depth):
+        copy = pltpu.make_async_copy(buf.at[b * 4 + slot], pieces_out.at[b], local_sems.at[7 + b])
+        copy.start()
+        out_copies.append(copy)
+    for m, (scr, out) in enumerate(((outw_s, outw_out), (inw_s, inw_out), (down_s, down_out))):
+        (offset, rows, blocks) = table[1 + m]
+        bring_rows(buf, flat, margin, offset, rows * blocks, piece_rows)
+        emit_matrix(flat, scr, margin, rows, blocks)
+        copy = pltpu.make_async_copy(scr, out, local_sems.at[4 + m])
+        copy.start()
+        out_copies.append(copy)
+
+    for b in range(depth):
+        for h in parts:
+
+            @pl.when((b <= z) & (z < depth - 1))
+            def _(b=b, h=h):
+                down(b, h).wait_send()
+
+            @pl.when((b >= z) & (z > 0))
+            def _(b=b, h=h):
+                up(b, h).wait_send()
+
+            side(b, h).wait_send()
+            for k in range(2):
+                twin(b, h, k).wait_send()
+    for copy in out_copies:
+        copy.wait()
+
+
+def start(own_rows, tokens, code_row, seg_col, table, tail_rows, padded, cuts, rows_q=256):
+    piece_rows = own_rows.shape[0]
+    half, width = tokens.shape
+    n = 2 * half
+    pairs = table[0][2]
+    local_width = pairs * LANES
+    hbm = pl.BlockSpec(memory_space=pl.ANY)
+    whole = pl.BlockSpec(memory_space=pltpu.VMEM)
+    mats = [jax.ShapeDtypeStruct((rows, blocks * LANES), bf16) for _, rows, blocks in table]
+    acts = [jax.ShapeDtypeStruct((n, local_width), bf16)] * 4
+    most = max(rows * blocks for _, rows, blocks in table)
+    parts = len(cuts)
+    dma = pltpu.SemaphoreType.DMA
+    return pl.pallas_call(
+        functools.partial(
+            start_kernel, piece_rows=piece_rows, tail_rows=tail_rows, table=table, cuts=cuts, rows_q=rows_q
+        ),
+        in_specs=[hbm, hbm, whole, whole],
+        out_specs=[hbm] * 5 + [whole] + [hbm] + [whole] * 5,
+        out_shape=mats
+        + [
+            jax.ShapeDtypeStruct((GROUPS, padded, LANES), bf16),
+            jax.ShapeDtypeStruct((tail_rows, LANES), f32),
+            jax.ShapeDtypeStruct((n, width), bf16),
+        ]
+        + acts
+        + [jax.ShapeDtypeStruct((pairs, 2, n), f32)],
+        scratch_shapes=[
+            pltpu.VMEM((piece_rows, LANES), f32),
+            pltpu.VMEM((4 * GROUPS, padded, LANES), bf16),
+            pltpu.VMEM((n, width), bf16),
+            pltpu.VMEM((most + 48, LANES), f32),
+        ]
+        + [pltpu.VMEM(m.shape, bf16) for m in mats]
+        + [
+            dma((GROUPS, parts)),
+            dma((GROUPS, parts)),
+            dma((GROUPS, parts)),
+            dma((GROUPS, parts)),
+            dma((GROUPS, parts)),
+            dma((2 * GROUPS, parts)),
+            dma((2 * GROUPS, parts)),
+            dma((2,)),
+            dma((11,)),
+        ],
+        cost_estimate=pl.CostEstimate(
+            flops=6 * n * width * local_width, bytes_accessed=60 << 20, transcendentals=8 * n * n
+        ),
+        compiler_params=params(collective_id=1, has_side_effects=True),
+        name="start",
+    )(own_rows, tokens, code_row, seg_col)
+
+
+def partner(block):
+    return lax.ppermute(block, "tensor", [(0, 1), (1, 0)])
+
+
+def both(own):
+    return jnp.concatenate([own, partner(own)], axis=0)
+
+
+def own_sum(partial):
+    half = partial.shape[0] // 2
+    return partial[:half].astype(f32) + partner(partial[half:].astype(bf16)).astype(f32)
+
+
+def local_fast(
+    tokens,
+    cotangent,
+    segment_ids,
+    padding,
+    shared_weights,
+    first_moment,
+    second_moment,
+    outer_momentum,
+):
+    me = lax.axis_index("tensor")
+    per = lax.axis_size("slot")
+    rows = tokens.shape[0]
+    local_width = D // 2
+    piece_rows = shared_weights.shape[1] // LANES
+    table, tail_at = matrix_table(2)
+    tail_rows = GROUPS * per * piece_rows - tail_at
+    padded = round_up(piece_rows + tail_rows, 16)
+
+    own_rows = shared_weights.reshape(piece_rows, 1, LANES)
+    seg = jnp.where(me == 0, segment_ids, jnp.roll(segment_ids, rows))
+    live = jnp.where(me == 0, padding, jnp.roll(padding, rows))
+    code = jnp.where(live == 1, seg, -1)
+    end = padded - round_up(2 * tail_rows + 16, 16)
+    marks = [end * i // 4 // 16 * 16 for i in range(4)] + [end, padded]
+    cuts = [(low, high - low) for low, high in zip(marks[:-1], marks[1:])]
+    (
+        proj_w, out_w, in_w, down_w, pieces, tail_all, x_all, query, keys, values, context, lse
+    ) = start(own_rows, tokens, code[None], seg[:, None], table, tail_rows, padded, cuts)
+    proj_w = proj_w.reshape(3, D, local_width)
+    flat_tail = tail_all.reshape(-1)
+    inner_bias = flat_tail[2 * local_width : 2 * local_width + FF // 2]
+    vec_own = flat_tail[2 * local_width + FF // 2 :].reshape(6, local_width)
+    vec_other = partner(vec_own)
+    vectors = jnp.where(
+        me == 0,
+        jnp.concatenate([vec_own, vec_other], axis=1),
+        jnp.concatenate([vec_other, vec_own], axis=1),
+    )
+
+    attn_sum = own_sum(jnp.dot(context, out_w, preferred_element_type=f32))
+    middle, normed_one, inv_one = layer_norm(
+        tokens.astype(f32) + (attn_sum + vectors[4]), vectors[0], vectors[1]
+    )
+    middle_all = both(middle.astype(bf16))
+    inner = jnp.dot(middle_all, in_w, preferred_element_type=f32) + inner_bias
+    activated = jax.nn.gelu(inner, approximate=False).astype(bf16)
+    ffn_sum = own_sum(jnp.dot(activated, down_w, preferred_element_type=f32))
+    result, normed_two, inv_two = layer_norm(
+        middle + (ffn_sum + vectors[5]), vectors[2], vectors[3]
+    )
+    block_out = result.astype(bf16)
+
+    grad_out = cotangent.astype(f32)
+    grad_gain_two = jnp.sum(grad_out * normed_two, axis=0)
+    grad_shift_two = jnp.sum(grad_out, axis=0)
+    grad_two = norm_back(grad_out * vectors[2], normed_two, inv_two)
+    grad_down_bias = jnp.sum(grad_two, axis=0)
+    back_all = both(grad_two.astype(bf16))
+    grad_down_w = row_contract(activated, back_all).astype(bf16)
+    grad_act = col_contract(back_all, down_w)
+    grad_inner = (grad_act * gelu_slope(inner)).astype(bf16)
+    grad_inner_bias = jnp.sum(grad_inner.astype(f32), axis=0)
+    grad_in_w = row_contract(middle_all, grad_inner).astype(bf16)
+    grad_middle = grad_two + own_sum(col_contract(grad_inner, in_w))
+    grad_gain_one = jnp.sum(grad_middle * normed_one, axis=0)
+    grad_shift_one = jnp.sum(grad_middle, axis=0)
+    grad_one = norm_back(grad_middle * vectors[0], normed_one, inv_one)
+    grad_out_bias = jnp.sum(grad_one, axis=0)
+    attn_back_all = both(grad_one.astype(bf16))
+    grad_out_w = row_contract(context, attn_back_all).astype(bf16)
+    grad_context = col_contract(attn_back_all, out_w).astype(bf16)
+    dq, dk, dv = attn_bwd(query, keys, values, context, grad_context, code[:, None], seg[None], lse)
+    grad_proj = jnp.stack([dq, dk, dv])
+    grad_proj_w = jnp.einsum("td,kte->kde", x_all, grad_proj, preferred_element_type=f32)
+    grad_query_bias = jnp.sum(dq.astype(f32), axis=0)
+    grad_value_bias = jnp.sum(dv.astype(f32), axis=0)
+    input_share = own_sum(jnp.einsum("kte,kde->td", grad_proj, proj_w, preferred_element_type=f32))
+    input_grad = (grad_one + input_share).astype(bf16)
+
+    vector_part = jnp.stack(
+        [
+            grad_gain_one,
+            grad_shift_one,
+            grad_gain_two,
+            grad_shift_two,
+            grad_out_bias,
+            grad_down_bias,
+        ]
+    )
+    halves = vector_part.reshape(6, 2, local_width)
+    vec_keep = jnp.where(me == 0, halves[:, 0], halves[:, 1])
+    vec_send = jnp.where(me == 0, halves[:, 1], halves[:, 0])
+    vector_grad = vec_keep + partner(vec_send)
+    tail_grad = jnp.concatenate(
+        [grad_query_bias, grad_value_bias, grad_inner_bias, vector_grad.reshape(-1)]
+    ).reshape(tail_rows, LANES)
+
+    matrices = [
+        grad_proj_w.astype(bf16).reshape(3 * D, local_width),
+        grad_out_w,
+        grad_in_w,
+        grad_down_w,
+    ]
+    short = round_up(piece_rows, 16)
+    slot = lax.axis_index("slot").astype(jnp.int32)
+    group = lax.axis_index("group")
+
+    def across(block, axis, bit):
+        return lax.ppermute(block, axis, [(i, i ^ bit) for i in range(lax.axis_size(axis))])
+
+    tail_sum = tail_grad + across(tail_grad, "slot", 1)
+    tail_sum = tail_sum + across(tail_sum, "slot", 2)
+
+    def blocked(state):
+        return state.reshape(GROUPS, piece_rows, LANES).transpose(1, 0, 2)
+
+    def unblocked(state):
+        return state.transpose(1, 0, 2).reshape(1, 1, GROUPS, piece_rows * LANES)
+
+    first = blocked(first_moment)
+    second = blocked(second_moment)
+    held = []
+    diffs = [None] * GROUPS
+    slot_word = slot.reshape(1)
+    for b in reversed(range(GROUPS)):
+        keep, send = flatten(b, slot_word, matrices, table, tail_at, tail_rows, per, piece_rows, short)
+        near = across(send, "slot", 1)
+        far = across((keep[1].astype(f32) + near[1].astype(f32)).astype(bf16), "slot", 2)
+        if b == GROUPS - 1:
+            there = far[piece_rows - tail_rows : piece_rows]
+            there = jnp.where(slot == per - 1, tail_sum.astype(bf16), there)
+            far = lax.dynamic_update_slice(far, there, (piece_rows - tail_rows, 0))
+        *held, diffs[b] = adamw(b, slot_word, keep, near, far, pieces, first, second, held, per, tail_at)
+
+    def turned(k):
+        picked = diffs[(GROUPS - 1) ^ k]
+        for z in range(GROUPS - 1):
+            picked = jnp.where(group == z, diffs[z ^ k], picked)
+        return picked
+
+    gathered = [turned(0)] + [across(turned(k), "group", k) for k in (1, 2, 3)]
+    mean_diff, new_momentum, new_weights = [
+        rows_out.reshape(1, piece_rows * LANES)
+        for rows_out in outer(gathered, own_rows, outer_momentum.reshape(piece_rows, 1, LANES))
+    ]
+    return (block_out, input_grad, *[unblocked(state) for state in held], mean_diff, new_momentum, new_weights)
+
+
 def solution(mesh):
+    dp = mesh.shape["dp"]
+    tensor_size = mesh.shape["tensor"]
+    piece = (4 * D * D + 2 * D * FF + 8 * D + FF) // tensor_size // dp
+    if tensor_size == 2 and piece % LANES == 0 and dp % GROUPS == 0:
+        mesh = Mesh(
+            mesh.devices.reshape(GROUPS, dp // GROUPS, tensor_size), ("group", "slot", "tensor")
+        )
+        data = ("group", "slot")
+        body = local_fast
+    else:
+        data = "dp"
+        body = local_general
+    every = ("group", "slot", "tensor") if body is local_fast else ("dp", "tensor")
     in_specs = (
-        P(("dp", "tensor"), None),
-        P(("dp", "tensor"), None),
-        P("dp"),
-        P("dp"),
-        P("tensor", "dp"),
-        P("tensor", "dp", None, None),
-        P("tensor", "dp", None, None),
-        P("tensor", "dp"),
+        P(every, None),
+        P(every, None),
+        P(data),
+        P(data),
+        P("tensor", data),
+        P("tensor", data, None, None),
+        P("tensor", data, None, None),
+        P("tensor", data),
     )
     out_specs = (
-        P(("dp", "tensor"), None),
-        P(("dp", "tensor"), None),
-        P("tensor", "dp", None, None),
-        P("tensor", "dp", None, None),
-        P("tensor", "dp", None, None),
-        P("tensor", "dp", None, None),
-        P("tensor", "dp"),
-        P("tensor", "dp"),
-        P("tensor", "dp"),
-    )
-    return jax.shard_map(local, mesh=mesh, in_specs=in_specs, out_specs=out_specs, check_vma=False)
+        P(every, None),
+        P(every, None),
+        P("tensor", data, None, None),
+        P("tensor", data, None, None),
+        P("tensor", data, None, None),
+        P("tensor", data, None, None),
+        P("tensor", data),
+        P("tensor", data),
+        P("tensor", data),
+    )
+    return jax.shard_map(body, mesh=mesh, in_specs=in_specs, out_specs=out_specs, check_vma=False)

time: 1810 us -> 566 us (0.31)
  other arithmetic: 505 us -> 30.1 us
  waiting for transfers between devices: 640 us -> 201 us
  local copies, waits for them, and re-layouts: 448 us -> 20.8 us
  Pallas kernels: 0 us -> 188 us
  matrix products: 171 us -> 79.7 us
  starting transfers between devices: 5.89 us -> 34.9 us
    all_gather x1 -> x0, other arithmetic: 265 us -> none  [local(): masters = lax.all_gather(shared_weights, 'dp', axis=1, tiled=True)[0]]
    pallas_call x0 -> x11, Pallas kernels: none -> 188 us  [the longest x1 98.7 us: start(): pl.pallas_call(functools.partial(start_kernel, piece_rows=piece_rows, tai...]
    all_gather x5 -> x0, waiting for transfers between devices: 183 us -> none  [the longest x1 131 us: local(): masters = lax.all_gather(shared_weights, 'dp', axis=1, tiled=True)[0]]
    ppermute x4 -> x22, waiting for transfers between devices: 365 us -> 201 us  [the longest x9 113 us: partner(): return lax.ppermute(block, 'tensor', [(0, 1), (1, 0)])]
    slice x8, local copies, waits for them, and re-layouts: 151 us -> 2.38 us  [the longest x4 1.58 us: own_sum(): partial[half:].astype(bf16)]
    dot_general x20 -> x5, matrix products: 134 us -> 42.6 us  [the longest x1 25 us: local_fast(): inner = jnp.dot(middle_all, in_w, preferred_element_type=f32) + inner_bias]
    reduce_scatter x5 -> x0, waiting for transfers between devices: 90.4 us -> none  [the longest x1 31.9 us: local(): lax.psum_scatter(jnp.dot(activated, down_weight, preferred_element_type=f...]
    dynamic_slice x1 -> x0, other arithmetic: 77.4 us -> none  [local(): lax.dynamic_index_in_dim(summed_grid, slot_index, 1, keepdims=False)]
  transfers between devices with their start and end apart: 14 -> 22, of which waited for: 9 -> 10; matrix products, arithmetic and copies ran while one was open for 33% -> 11% of each run, Pallas kernels for 0% -> 15%
where the time goes in v1:
time: 566 us; the launch traced here: 555 us
  waiting for transfers between devices  201 us (36%)
  Pallas kernels  188 us (33%)
  matrix products  79.7 us (14%)
  starting transfers between devices  34.9 us (6%)
  other arithmetic  30.1 us (5%)
  local copies, waits for them, and re-layouts  20.8 us (4%)
    ppermute x9, waiting for transfers between devices, partner(): return lax.ppermute(block, 'tensor', [(0, 1), (1, 0)])  113 us
    pallas_call x1, Pallas kernels, start(): pl.pallas_call(functools.partial(start_kernel, piece_rows=piece_rows, tai...  98.7 us
    ppermute x13, waiting for transfers between devices, across(): lax.ppermute(block, axis, [(i, i ^ bit) for i in range(lax.axis_size(axis...  87.7 us
    pallas_call x4, Pallas kernels, adamw(): pl.pallas_call(functools.partial(adamw_kernel, b=b, piece_rows=piece_rows...  29.5 us
    pallas_call x4, Pallas kernels, flatten(): pl.pallas_call(functools.partial(flatten_kernel, segments=segments, skip=...  27 us
    pallas_call x1, Pallas kernels, attn_bwd(): pl.pallas_call(functools.partial(attn_bwd_kernel, rows_q=rows_q), grid=(p...  26.8 us
    ppermute x13, starting transfers between devices, across(): lax.ppermute(block, axis, [(i, i ^ bit) for i in range(lax.axis_size(axis...  26.3 us
    dot_general x1, matrix products, local_fast(): inner = jnp.dot(middle_all, in_w, preferred_element_type=f32) + inner_bias  25 us
  transfers between devices with their start and end apart: 22, of which 10 were waited for; matrix products, arithmetic and copies ran while one was open for 11% of the time, Pallas kernels for 15%

profile of v1, /device:TPU:8, one launch (start us, length us, event | category | flops | bytes accessed | tf_op | source)
XLA Modules:
  0.0 555.3 jit_solution(7839930623307304321)
XLA Ops:
  1.4 1.3 fusion.39
  2.7 1.0 copy.34.seg_ref
  3.7 98.7 %start.1 = (bf16[3072,512]{1,0:T(8,128)(2,1)}, bf16[512,1024]{1,0:T(8,128)(2,1)}, bf16[1024,2048]{1,0:T(8,128)(2,1)}, bf16[2048,1024]{1,0:T(8,128)(2,1)}, bf16[4...) custom-call(f32[3075,1,128]{2,1,0:T(1,128)} %bitcast.99, ...), custom_call_target="tpu_custom_call" | custom-call | flops 3221225472 | bytes 62914560 | tf_op jit(solution)/shard_map/start/pallas_call | solution.py:1062
  102.5 2.9 fusion.61
  105.4 2.0 copy-done.10
  108.4 1.3 collective-permute-start.1
  109.7 23.4 %collective-permute-done.1 = f32[6,512]{1,0:T(8,128)S(1)} collective-permute-done((f32[6,512]{1,0:T(8,128)S(1)}, f32[6,512]{1,0:T(8,128)S(1)}, u32[]{:S(2)}, u32[]{:S(2)}) %collective-permute-start.1) | collective-permute-done | bytes 12320 | tf_op jit(solution)/shard_map/ppermute | solution.py:1103
  133.2 1.0 copy-done.13
  134.2 2.4 fusion.55
  138.3 23.5 %collective-permute-done.2 = bf16[512,1024]{1,0:T(8,128)(2,1)S(1)} collective-permute-done((bf16[512,1024]{1,0:T(8,128)(2,1)S(1)}, bf16[512,1024]{1,0:T(8,128)(2,1)S(1)}, u32[]{:S(2)}, u32[]{:S(2)}) %collective-permute-start.2) | collective-permute-done | bytes 1048608 | tf_op jit(solution)/shard_map/ppermute | solution.py:1103
  161.8 25.0 %fusion.2 = (bf16[1024,2048]{1,0:T(8,128)(2,1)S(1)}, f32[1024,2048]{1,0:T(8,128)}) fusion(f32[2048]{0:T(1024)S(1)} %slice_bitcast_fusion, bf16[1024,2048]{1,0:T(8,128)(2,1)S(1)} %copy-done.32, bf16[512,1024]{1,0:T(8,128)(2,1)S(1)} %collective-permute-done.2, bf16[512,1024]{1,0:T(8,128)(2,1)S(1)} %fusion.31), kind=kOutput, calls=%fused_computation.4 | convolution fusion | flops 4437573632 | bytes 18882560 | tf_op jit(solution)/shard_map/dot_general | solution.py:1160
  186.8 4.5 fusion.62
  192.4 22.6 %collective-permute-done.3 = bf16[512,1024]{1,0:T(8,128)(2,1)S(1)} collective-permute-done((bf16[512,1024]{1,0:T(8,128)(2,1)S(1)}, bf16[512,1024]{1,0:T(8,128)(2,1)S(1)}, u32[]{:S(2)}, u32[]{:S(2)}) %collective-permute-start.3) | collective-permute-done | bytes 1048608 | tf_op jit(solution)/shard_map/ppermute | solution.py:1103
  216.2 1.0 fusion.22
  217.2 1.9 fusion.49
  219.1 1.3 copy-done.1
  221.4 21.8 %collective-permute-done.4 = bf16[512,1024]{1,0:T(8,128)(2,1)} collective-permute-done((bf16[512,1024]{1,0:T(8,128)(2,1)S(1)}, bf16[512,1024]{1,0:T(8,128)(2,1)}, u32[]{:S(2)}, u32[]{:S(2)}) %collective-permute-start.4) | collective-permute-done | bytes 1048608 | tf_op jit(solution)/shard_map/ppermute | solution.py:1103
  243.2 11.3 %convert_reduce_fusion = (f32[2048]{0:T(1024)S(1)}, bf16[1024,2048]{1,0:T(8,128)(2,1)S(1)}) fusion(f32[1024,2048]{1,0:T(8,128)} %get-tuple-element.138, f32[2048]{0:T(1024)S(1)} %slice_bitcast_fusion, bf16[2048,1024]{1,0:T(8,128)(2,1)} %get-tuple-element.59, bf16[512,1024]{1,0:T(8,128)(2,1)} %collective-permute-done.4, ...), kind=kOutput, calls=%fused_computation.11 | convolution fusion | flops 4326422528 | bytes 18890752 | tf_op jit(solution)/shard_map/dot_general | solution.py:92
  254.6 4.5 fusion.63
  259.2 2.0 copy-done.11
  261.2 1.1 slice.192
  263.1 6.3 %convolution_convert_fusion.1.refs_1_.refs_0_ = bf16[1024,2048]{1,0:T(8,128)(2,1)} fusion(bf16[1024,2048]{1,0:T(8,128)(2,1)S(1)} %get-tuple-element.140, bf16[512,1024]{1,0:T(8,128)(2,1)S(1)} %copy-done.29, bf16[512,1024]{1,0:T(8,128)(2,1)S(1)} %copy-done.15), kind=kOutput, calls=%fused_computation.28 | convolution fusion | flops 4301258752 | bytes 10485760 | tf_op jit(solution)/shard_map/dot_general | solution.py:86
  269.4 7.4 %convolution_convert_fusion.refs_1_.refs_0_ = bf16[2048,1024]{1,0:T(8,128)(2,1)} fusion(bf16[1024,2048]{1,0:T(8,128)(2,1)S(1)} %copy-done.36, bf16[512,1024]{1,0:T(8,128)(2,1)} %collective-permute-done.4, bf16[512,1024]{1,0:T(8,128)(2,1)S(1)} %convert_element_type.136), kind=kOutput, calls=%fused_computation.27 | convolution fusion | flops 4301258752 | bytes 10485760 | tf_op jit(solution)/shard_map/dot_general | solution.py:86
  276.8 8.5 %flatten_2.1 = (bf16[2,3088,128]{2,1,0:T(8,128)(2,1)}, bf16[2,3088,128]{2,1,0:T(8,128)(2,1)}) custom-call(s32[1]{0:T(128)} %bitcast.17.slot_ref, bf16[1024,2048]{1,0:T(8,128)(2,1)} %convolution_convert_fusion.1.refs_1_.refs_0_, bf16[2048,1024]{1,0:T(8,128)(2,1)} %convolution_convert_fusion.refs_1_.refs_0_), custom_call_target="tpu_custom_call" | custom-call | flops 1574400 | bytes 9446400 | tf_op jit(solution)/shard_map/flatten_2/pallas_call | solution.py:541
  285.2 3.0 multiply_reduce_fusion
  288.3 2.0 fusion.51
  290.4 1.3 collective-permute-start.16
  291.7 1.0 copy.35.code_ref
  292.7 6.3 %flatten_3.1 = (bf16[2,3088,128]{2,1,0:T(8,128)(2,1)}, bf16[2,3088,128]{2,1,0:T(8,128)(2,1)}) custom-call(s32[1]{0:T(128)} %bitcast.17.slot_ref, bf16[2048,1024]{1,0:T(8,128)(2,1)} %convolution_convert_fusion.refs_1_.refs_0_), custom_call_target="tpu_custom_call" | custom-call | flops 1574400 | bytes 9446400 | tf_op jit(solution)/shard_map/flatten_3/pallas_call | solution.py:541
  300.3 2.5 fusion.35
  303.3 21.6 %collective-permute-done.6 = bf16[512,1024]{1,0:T(8,128)(2,1)} collective-permute-done((bf16[512,1024]{1,0:T(8,128)(2,1)S(1)}, bf16[512,1024]{1,0:T(8,128)(2,1)}, u32[]{:S(2)}, u32[]{:S(2)}) %collective-permute-start.6) | collective-permute-done | bytes 1048608 | tf_op jit(solution)/shard_map/ppermute | solution.py:1103
  324.9 3.8 convolution_convert_fusion.3.dctx_ref
  328.7 26.8 %attn_bwd.1 = (bf16[1024,512]{1,0:T(8,128)(2,1)}, bf16[1024,512]{1,0:T(8,128)(2,1)}, bf16[1024,512]{1,0:T(8,128)(2,1)}) custom-call(bf16[1024,512]{1,0:T(8,128)(2,1)} %get-tuple-element.60.q_ref, bf16[1024,512]{1,0:T(8,128)(2,1)} %get-tuple-element.61.k_ref, bf16[1024,512]{1,0:T(8,128)(2,1)} %get-tuple-element.62.v_ref, ...), custom_call_target="tpu_custom_call" | custom-call | flops 10737418240 | bytes 8388608 | tf_op jit(solution)/shard_map/attn_bwd/pallas_call | solution.py:450
  355.5 6.7 %convert_bitcast_fusion = bf16[3,1024,512]{1,2,0:T(8,128)(2,1)} fusion(bf16[1024,1024]{1,0:T(8,128)(2,1)S(1)} %copy-done.37, bf16[1,1024,512]{2,1,0:T(8,128)(2,1)} %bitcast.104, bf16[1,1024,512]{2,1,0:T(8,128)(2,1)} %bitcast.132, bf16[1,1024,512]{2,1,0:T(8,128)(2,1)} %bitcast.102), kind=kOutput, calls=%fused_computation.30 | convolution fusion | flops 3225944064 | bytes 8388608 | tf_op jit(solution)/shard_map/td,kte->kde/dot_general | solution.py:1189
  362.2 4.6 copy.37
  366.8 3.8 convolution_convert_fusion.2.refs_1_.refs_0_
  370.6 5.1 flatten_0.1
  375.8 7.1 %flatten_1.1 = (bf16[2,3088,128]{2,1,0:T(8,128)(2,1)}, bf16[2,3088,128]{2,1,0:T(8,128)(2,1)}) custom-call(s32[1]{0:T(128)} %bitcast.17.slot_ref, bf16[512,1024]{1,0:T(8,128)(2,1)} %convolution_convert_fusion.2.refs_1_.refs_0_, bf16[1024,2048]{1,0:T(8,128)(2,1)} %convolution_convert_fusion.1.refs_1_.refs_0_), custom_call_target="tpu_custom_call" | custom-call | flops 1574400 | bytes 9446400 | tf_op jit(solution)/shard_map/flatten_1/pallas_call | solution.py:541
  383.3 1.5 convert_reduce_fusion.2
  384.8 1.6 convert_reduce_fusion.3
  386.6 1.7 fusion.36
  388.9 1.6 collective-permute-start.18
  390.5 2.2 fusion.33
  393.3 1.3 fusion.34
  394.7 1.5 collective-permute-start.11
  396.2 3.5 convolution_bitcast_fusion
  399.7 1.9 copy-done.8
  401.8 7.6 %collective-permute-done.18 = f32[48,128]{1,0:T(8,128)S(1)} collective-permute-done((f32[48,128]{1,0:T(8,128)S(1)}, f32[48,128]{1,0:T(8,128)S(1)}, u32[]{:S(2)}, u32[]{:S(2)}) %collective-permute-start.18) | collective-permute-done | bytes 24608 | tf_op jit(solution)/shard_map/ppermute | solution.py:1224
  410.2 0.9 copy-done.18
  411.1 1.4 dynamic_update_slice.3.far
  412.5 7.4 %adamw_3.1 = (f32[3075,4,128]{2,1,0:T(4,128)}, f32[3075,4,128]{2,1,0:T(4,128)}, f32[3075,4,128]{2,1,0:T(4,128)}, f32[3075,4,128]{2,1,0:T(4,128)}, bf16[3088,128]{1,0:T(8,128)(2,1)}) custom-call(s32[1]{0:T(128)} %bitcast.17.slot_ref, bf16[2,3088,128]{2,1,0:T(8,128)(2,1)} %get-tuple-element.76.keep, bf16[2,3088,128]{2,1,0:T(8,128)(2,1)} %collective-permute-done.14.near, ...), custom_call_target="tpu_custom_call" | custom-call | flops 11808000 | bytes 11808000 | tf_op jit(solution)/shard_map/adamw_3/pallas_call | solution.py:636
  419.9 7.3 %adamw_2.1 = (f32[3075,4,128]{2,1,0:T(4,128)}, f32[3075,4,128]{2,1,0:T(4,128)}, f32[3075,4,128]{2,1,0:T(4,128)}, f32[3075,4,128]{2,1,0:T(4,128)}, bf16[3088,128]{1,0:T(8,128)(2,1)}) custom-call(s32[1]{0:T(128)} %bitcast.17.slot_ref, ...), custom_call_target="tpu_custom_call", output_to_operand_aliasing={{0}: (7, {}), {1}: (8, {}), {2}: (9, {}), {3}: (10, {})} | custom-call | flops 11808000 | bytes 11808000 | tf_op jit(solution)/shard_map/adamw_2/pallas_call | solution.py:636
  427.2 15.3 %collective-permute-done.11.far = bf16[3088,128]{1,0:T(8,128)(2,1)} collective-permute-done((bf16[3088,128]{1,0:T(8,128)(2,1)}, bf16[3088,128]{1,0:T(8,128)(2,1)}, u32[]{:S(2)}, u32[]{:S(2)}) %collective-permute-start.11) | collective-permute-done | bytes 790560 | tf_op jit(solution)/shard_map/ppermute | solution.py:1224
  442.5 7.3 %adamw_1.1 = (f32[3075,4,128]{2,1,0:T(4,128)}, f32[3075,4,128]{2,1,0:T(4,128)}, f32[3075,4,128]{2,1,0:T(4,128)}, f32[3075,4,128]{2,1,0:T(4,128)}, bf16[3088,128]{1,0:T(8,128)(2,1)}) custom-call(s32[1]{0:T(128)} %bitcast.17.slot_ref, ...), custom_call_target="tpu_custom_call", output_to_operand_aliasing={{0}: (7, {}), {1}: (8, {}), {2}: (9, {}), {3}: (10, {})} | custom-call | flops 11808000 | bytes 11808000 | tf_op jit(solution)/shard_map/adamw_1/pallas_call | solution.py:636
  449.9 7.5 %adamw_0.1 = (f32[3075,4,128]{2,1,0:T(4,128)}, f32[3075,4,128]{2,1,0:T(4,128)}, f32[3075,4,128]{2,1,0:T(4,128)}, f32[3075,4,128]{2,1,0:T(4,128)}, bf16[3088,128]{1,0:T(8,128)(2,1)}) custom-call(s32[1]{0:T(128)} %bitcast.17.slot_ref, ...), custom_call_target="tpu_custom_call", output_to_operand_aliasing={{0}: (7, {}), {1}: (8, {}), {2}: (9, {}), {3}: (10, {})} | custom-call | flops 11808000 | bytes 11808000 | tf_op jit(solution)/shard_map/adamw_0/pallas_call | solution.py:636
  457.4 2.5 select_select_fusion
  460.0 9.7 %collective-permute-start.19 = (bf16[3088,128]{1,0:T(8,128)(2,1)S(1)}, bf16[3088,128]{1,0:T(8,128)(2,1)S(1)}, u32[]{:S(2)}, u32[]{:S(2)}) collective-permute-start(bf16[3088,128]{1,0:T(8,128)(2,1)S(1)} %get-tuple-element.122), channel_id=1, source_target_pairs={{0,8},{8,0},{16,24},{24,16},{1,9},{9,1},{17,25},{25,17},{2,10},{10... | collective-permute-start | bytes 2371592 | tf_op jit(solution)/shard_map/ppermute | solution.py:1224
  469.7 10.6 %collective-permute-start.20 = (bf16[3088,128]{1,0:T(8,128)(2,1)S(1)}, bf16[3088,128]{1,0:T(8,128)(2,1)S(1)}, u32[]{:S(2)}, u32[]{:S(2)}) collective-permute-start(bf16[3088,128]{1,0:T(8,128)(2,1)S(1)} %get-tuple-element.121), channel_id=1, source_target_pairs={{0,16},{8,24},{16,0},{24,8},{1,17},{9,25},{17,1},{25,9},{2,18},{10... | collective-permute-start | bytes 2371592 | tf_op jit(solution)/shard_map/ppermute | solution.py:1224
  480.9 2.8 fusion.24
  483.7 18.3 %collective-permute-done.19.d1 = bf16[3088,128]{1,0:T(8,128)(2,1)S(1)} collective-permute-done((bf16[3088,128]{1,0:T(8,128)(2,1)S(1)}, bf16[3088,128]{1,0:T(8,128)(2,1)S(1)}, u32[]{:S(2)}, u32[]{:S(2)}) %collective-permute-start.19) | collective-permute-done | bytes 790560 | tf_op jit(solution)/shard_map/ppermute | solution.py:1224
  502.0 30.3 %collective-permute-done.20.d2 = bf16[3088,128]{1,0:T(8,128)(2,1)S(1)} collective-permute-done((bf16[3088,128]{1,0:T(8,128)(2,1)S(1)}, bf16[3088,128]{1,0:T(8,128)(2,1)S(1)}, u32[]{:S(2)}, u32[]{:S(2)}) %collective-permute-start.20) | collective-permute-done | bytes 790560 | tf_op jit(solution)/shard_map/ppermute | solution.py:1224
  532.3 16.2 %collective-permute-done.21.d3 = bf16[3088,128]{1,0:T(8,128)(2,1)S(1)} collective-permute-done((bf16[3088,128]{1,0:T(8,128)(2,1)S(1)}, bf16[3088,128]{1,0:T(8,128)(2,1)S(1)}, u32[]{:S(2)}, u32[]{:S(2)}) %collective-permute-start.21) | collective-permute-done | bytes 790560 | tf_op jit(solution)/shard_map/ppermute | solution.py:1224
  548.5 0.9 copy-done.24
  549.4 5.7 %outer_step.1 = (f32[3075,1,128]{2,1,0:T(1,128)}, f32[3075,1,128]{2,1,0:T(1,128)}, f32[3075,1,128]{2,1,0:T(1,128)}) custom-call(bf16[3088,128]{1,0:T(8,128)(2,1)} %get-tuple-element.123.d0, bf16[3088,128]{1,0:T(8,128)(2,1)} %copy-done.22, bf16[3088,128]{1,0:T(8,128)(2,1)} %copy-done.23, bf16[3088,128]{1,0:T(8,128)(2,1)} %copy-done.24, ...), custom_call_target="tpu_custom_call" | custom-call | tf_op jit(solution)/shard_map/outer_step/pallas_call | solution.py:709
  (129 shorter events, 12.9 us)
Async XLA Ops:
  2.7 99.8 %copy-start.26 = (s32[1024]{0:T(1024)}, s32[1024]{0:T(1024)S(1)}, u32[]{:S(2)}) copy-start(s32[1024]{0:T(1024)S(1)} %get-tuple-element.119) | copy-start | bytes 12292
  102.5 5.9 %copy-start.25 = (f32[48,128]{1,0:T(8,128)S(1)}, f32[48,128]{1,0:T(8,128)}, u32[]{:S(2)}) copy-start(f32[48,128]{1,0:T(8,128)} %get-tuple-element.57) | copy-start | bytes 73732
  102.5 31.7 %copy-start.12 = (bf16[512,1024]{1,0:T(8,128)(2,1)S(1)}, bf16[512,1024]{1,0:T(8,128)(2,1)}, u32[]{:S(2)}) copy-start(bf16[512,1024]{1,0:T(8,128)(2,1)} %tokens_hbm.1) | copy-start | bytes 3145732
  105.4 2.0 copy-start.10
  107.6 25.6 %collective-permute-start = (bf16[512,1024]{1,0:T(8,128)(2,1)S(1)}, bf16[512,1024]{1,0:T(8,128)(2,1)S(1)}, u32[]{:S(2)}, u32[]{:S(2)}) collective-permute-start(bf16[512,1024]{1,0:T(8,128)(2,1)S(1)} %slice.194), channel_id=1, source_target_pairs={{0,1},{1,0},{2,3},{3,2},{4,5},{5,4},{6,7},{7,6},{8,9},{9,8},{10,11... | collective-permute-start | bytes 3145736 | tf_op jit(solution)/shard_map/ppermute | solution.py:1103
  108.4 24.7 %collective-permute-start.1 = (f32[6,512]{1,0:T(8,128)S(1)}, f32[6,512]{1,0:T(8,128)S(1)}, u32[]{:S(2)}, u32[]{:S(2)}) collective-permute-start(f32[6,512]{1,0:T(8,128)S(1)} %reshape.149), channel_id=1, source_target_pairs={{0,1},{1,0},{2,3},{3,2},{4,5},{5,4},{6,7},{7,6},{8,9},{9,8},{10,11... | collective-permute-start | bytes 36872 | tf_op jit(solution)/shard_map/ppermute | solution.py:1103
  133.2 1.0 copy-start.13
  136.6 25.2 %copy-start.32 = (bf16[1024,2048]{1,0:T(8,128)(2,1)S(1)}, bf16[1024,2048]{1,0:T(8,128)(2,1)}, u32[]{:S(2)}) copy-start(bf16[1024,2048]{1,0:T(8,128)(2,1)} %get-tuple-element.58) | copy-start | bytes 12582916
  137.4 49.4 %copy-start.14 = (bf16[512,1024]{1,0:T(8,128)(2,1)}, bf16[512,1024]{1,0:T(8,128)(2,1)S(1)}, u32[]{:S(2)}) copy-start(bf16[512,1024]{1,0:T(8,128)(2,1)S(1)} %fusion.31) | copy-start | bytes 3145732
  137.4 24.4 %collective-permute-start.2 = (bf16[512,1024]{1,0:T(8,128)(2,1)S(1)}, bf16[512,1024]{1,0:T(8,128)(2,1)S(1)}, u32[]{:S(2)}, u32[]{:S(2)}) collective-permute-start(bf16[512,1024]{1,0:T(8,128)(2,1)S(1)} %fusion.31), channel_id=1, source_target_pairs={{0,1},{1,0},{2,3},{3,2},{4,5},{5,4},{6,7},{7,6},{8,9},{9,8},{10,11... | collective-permute-start | bytes 3145736 | tf_op jit(solution)/shard_map/ppermute | solution.py:1103
  161.8 25.0 %copy-start.28 = (bf16[512,1024]{1,0:T(8,128)(2,1)}, bf16[512,1024]{1,0:T(8,128)(2,1)S(1)}, u32[]{:S(2)}) copy-start(bf16[512,1024]{1,0:T(8,128)(2,1)S(1)} %collective-permute-done.2) | copy-start | bytes 3145732
  161.8 25.0 %copy-start.34 = (bf16[2048,1024]{1,0:T(8,128)(2,1)S(1)}, bf16[2048,1024]{1,0:T(8,128)(2,1)}, u32[]{:S(2)}) copy-start(bf16[2048,1024]{1,0:T(8,128)(2,1)} %get-tuple-element.59) | copy-start | bytes 12582916
  186.8 4.5 copy-start.35
  191.5 23.5 %collective-permute-start.3 = (bf16[512,1024]{1,0:T(8,128)(2,1)S(1)}, bf16[512,1024]{1,0:T(8,128)(2,1)S(1)}, u32[]{:S(2)}, u32[]{:S(2)}) collective-permute-start(bf16[512,1024]{1,0:T(8,128)(2,1)S(1)} %slice.193), channel_id=1, source_target_pairs={{0,1},{1,0},{2,3},{3,2},{4,5},{5,4},{6,7},{7,6},{8,9},{9,8},{10,11... | collective-permute-start | bytes 3145736 | tf_op jit(solution)/shard_map/ppermute | solution.py:1103
  215.0 1.3 copy-start.3
  219.1 1.3 copy-start.1
  220.6 22.7 %collective-permute-start.4 = (bf16[512,1024]{1,0:T(8,128)(2,1)S(1)}, bf16[512,1024]{1,0:T(8,128)(2,1)}, u32[]{:S(2)}, u32[]{:S(2)}) collective-permute-start(bf16[512,1024]{1,0:T(8,128)(2,1)S(1)} %convert_element_type.136), channel_id=1, source_target_pairs={{0,1},{1,0},{2,3},{3,2},{4,5},{5,4},{6,7},{7,6},{8,9},{9,8},{10,11... | collective-permute-start | bytes 3145736 | tf_op jit(solution)/shard_map/ppermute | solution.py:1103
  243.2 11.4 %copy-start.33 = (bf16[1024,2048]{1,0:T(8,128)(2,1)S(1)}, bf16[1024,2048]{1,0:T(8,128)(2,1)}, u32[]{:S(2)}) copy-start(bf16[1024,2048]{1,0:T(8,128)(2,1)} %get-tuple-element.58) | copy-start | bytes 12582916
  254.6 8.5 %copy-start.15 = (bf16[512,1024]{1,0:T(8,128)(2,1)S(1)}, bf16[512,1024]{1,0:T(8,128)(2,1)}, u32[]{:S(2)}) copy-start(bf16[512,1024]{1,0:T(8,128)(2,1)} %copy-done.14) | copy-start | bytes 3145732
  254.6 8.5 %copy-start.29 = (bf16[512,1024]{1,0:T(8,128)(2,1)S(1)}, bf16[512,1024]{1,0:T(8,128)(2,1)}, u32[]{:S(2)}) copy-start(bf16[512,1024]{1,0:T(8,128)(2,1)} %copy-done.28) | copy-start | bytes 3145732
  259.1 2.0 copy-start.11
  262.3 7.1 %copy-start.36 = (bf16[1024,2048]{1,0:T(8,128)(2,1)S(1)}, bf16[1024,2048]{1,0:T(8,128)(2,1)}, u32[]{:S(2)}) copy-start(bf16[1024,2048]{1,0:T(8,128)(2,1)} %copy-done.35) | copy-start | bytes 12582916
  262.3 22.9 %collective-permute-start.5 = (bf16[512,1024]{1,0:T(8,128)(2,1)}, bf16[512,1024]{1,0:T(8,128)(2,1)}, u32[]{:S(2)}, u32[]{:S(2)}) collective-permute-start(bf16[512,1024]{1,0:T(8,128)(2,1)} %slice.192), channel_id=1, source_target_pairs={{0,1},{1,0},{2,3},{3,2},{4,5},{5,4},{6,7},{7,6},{8,9},{9,8},{10,11... | collective-permute-start | bytes 3145736 | tf_op jit(solution)/shard_map/ppermute | solution.py:1103
  276.7 8.5 %copy-start.2 = (f32[512,1024]{1,0:T(8,128)S(1)}, f32[512,1024]{1,0:T(8,128)}, u32[]{:S(2)}) copy-start(f32[512,1024]{1,0:T(8,128)} %copy-done.1) | copy-start | bytes 6291460
  285.2 15.0 %collective-permute-start.12 = (bf16[2,3088,128]{2,1,0:T(8,128)(2,1)}, bf16[2,3088,128]{2,1,0:T(8,128)(2,1)}, u32[]{:S(2)}, u32[]{:S(2)}) collective-permute-start(bf16[2,3088,128]{2,1,0:T(8,128)(2,1)} %get-tuple-element.75), channel_id=1, source_target_pairs={{0,2},{2,0},{4,6},{6,4},{1,3},{3,1},{5,7},{7,5},{8,10},{10,8},{12,... | collective-permute-start | bytes 4743176 | tf_op jit(solution)/shard_map/ppermute | solution.py:1224
  288.3 3.4 copy-start.27
  290.3 8.9 %copy-start = (f32[512,1024]{1,0:T(8,128)S(1)}, f32[512,1024]{1,0:T(8,128)}, u32[]{:S(2)}) copy-start(f32[512,1024]{1,0:T(8,128)} %get-tuple-element.112) | copy-start | bytes 6291460
  290.4 9.9 %collective-permute-start.16 = (f32[6,512]{1,0:T(8,128)S(1)}, f32[6,512]{1,0:T(8,128)S(1)}, u32[]{:S(2)}, u32[]{:S(2)}) collective-permute-start(f32[6,512]{1,0:T(8,128)S(1)} %bitcast.125), channel_id=1, source_target_pairs={{0,1},{1,0},{2,3},{3,2},{4,5},{5,4},{6,7},{7,6},{8,9},{9,8},{10,11... | collective-permute-start | bytes 36872 | tf_op jit(solution)/shard_map/ppermute | solution.py:1103
  299.0 87.6 %collective-permute-start.14 = (bf16[2,3088,128]{2,1,0:T(8,128)(2,1)}, bf16[2,3088,128]{2,1,0:T(8,128)(2,1)}, u32[]{:S(2)}, u32[]{:S(2)}) collective-permute-start(bf16[2,3088,128]{2,1,0:T(8,128)(2,1)} %get-tuple-element.77), channel_id=1, source_target_pairs={{0,2},{2,0},{4,6},{6,4},{1,3},{3,1},{5,7},{7,5},{8,10},{10,8},{12,... | collective-permute-start | bytes 4743176 | tf_op jit(solution)/shard_map/ppermute | solution.py:1224
  299.4 25.5 %collective-permute-start.6 = (bf16[512,1024]{1,0:T(8,128)(2,1)S(1)}, bf16[512,1024]{1,0:T(8,128)(2,1)}, u32[]{:S(2)}, u32[]{:S(2)}) collective-permute-start(bf16[512,1024]{1,0:T(8,128)(2,1)S(1)} %convert_element_type.139), channel_id=1, source_target_pairs={{0,1},{1,0},{2,3},{3,2},{4,5},{5,4},{6,7},{7,6},{8,9},{9,8},{10,11... | collective-permute-start | bytes 3145736 | tf_op jit(solution)/shard_map/ppermute | solution.py:1103
  302.8 117.1 %collective-permute-start.13 = (bf16[3088,128]{1,0:T(8,128)(2,1)}, bf16[3088,128]{1,0:T(8,128)(2,1)}, u32[]{:S(2)}, u32[]{:S(2)}) collective-permute-start(bf16[3088,128]{1,0:T(8,128)(2,1)} %fusion.35), channel_id=1, source_target_pairs={{0,4},{2,6},{4,0},{6,2},{1,5},{3,7},{5,1},{7,3},{8,12},{10,14},{12... | collective-permute-start | bytes 2371592 | tf_op jit(solution)/shard_map/ppermute | solution.py:1224
  328.7 26.8 %copy-start.37 = (bf16[1024,1024]{1,0:T(8,128)(2,1)S(1)}, bf16[1024,1024]{1,0:T(8,128)(2,1)}, u32[]{:S(2)}) copy-start(bf16[1024,1024]{1,0:T(8,128)(2,1)} %get-tuple-element.68) | copy-start | bytes 6291460
  375.8 10.9 %copy-start.4 = (bf16[2,3088,128]{2,1,0:T(8,128)(2,1)S(1)}, bf16[2,3088,128]{2,1,0:T(8,128)(2,1)}, u32[]{:S(2)}) copy-start(bf16[2,3088,128]{2,1,0:T(8,128)(2,1)} %get-tuple-element.76.keep) | copy-start | bytes 4743172
  375.8 14.7 %copy-start.5 = (bf16[2,3088,128]{2,1,0:T(8,128)(2,1)S(1)}, bf16[2,3088,128]{2,1,0:T(8,128)(2,1)}, u32[]{:S(2)}) copy-start(bf16[2,3088,128]{2,1,0:T(8,128)(2,1)} %get-tuple-element.69.keep) | copy-start | bytes 4743172
  375.8 14.7 %collective-permute-start.8 = (bf16[2,3088,128]{2,1,0:T(8,128)(2,1)}, bf16[2,3088,128]{2,1,0:T(8,128)(2,1)}, u32[]{:S(2)}, u32[]{:S(2)}) collective-permute-start(bf16[2,3088,128]{2,1,0:T(8,128)(2,1)} %get-tuple-element.70), channel_id=1, source_target_pairs={{0,2},{2,0},{4,6},{6,4},{1,3},{3,1},{5,7},{7,5},{8,10},{10,8},{12,... | collective-permute-start | bytes 4743176 | tf_op jit(solution)/shard_map/ppermute | solution.py:1224
  382.9 10.4 %copy-start.6 = (bf16[2,3088,128]{2,1,0:T(8,128)(2,1)S(1)}, bf16[2,3088,128]{2,1,0:T(8,128)(2,1)}, u32[]{:S(2)}) copy-start(bf16[2,3088,128]{2,1,0:T(8,128)(2,1)} %get-tuple-element.72.keep) | copy-start | bytes 4743172
  382.9 10.3 %collective-permute-start.10 = (bf16[2,3088,128]{2,1,0:T(8,128)(2,1)}, bf16[2,3088,128]{2,1,0:T(8,128)(2,1)S(1)}, u32[]{:S(2)}, u32[]{:S(2)}) collective-permute-start(bf16[2,3088,128]{2,1,0:T(8,128)(2,1)} %get-tuple-element.73), channel_id=1, source_target_pairs={{0,2},{2,0},{4,6},{6,4},{1,3},{3,1},{5,7},{7,5},{8,10},{10,8},{12,... | collective-permute-start | bytes 4743176 | tf_op jit(solution)/shard_map/ppermute | solution.py:1224
  384.8 11.4 %copy-start.16 = (bf16[1024,512]{1,0:T(8,128)(2,1)S(1)}, bf16[1024,512]{1,0:T(8,128)(2,1)}, u32[]{:S(2)}) copy-start(bf16[1024,512]{1,0:T(8,128)(2,1)} %get-tuple-element.64) | copy-start | bytes 3145732
  384.8 11.4 %copy-start.17 = (bf16[1024,512]{1,0:T(8,128)(2,1)S(1)}, bf16[1024,512]{1,0:T(8,128)(2,1)}, u32[]{:S(2)}) copy-start(bf16[1024,512]{1,0:T(8,128)(2,1)} %get-tuple-element.66) | copy-start | bytes 3145732
  384.8 11.4 %copy-start.30 = (bf16[3072,512]{1,0:T(8,128)(2,1)S(1)}, bf16[3072,512]{1,0:T(8,128)(2,1)}, u32[]{:S(2)}) copy-start(bf16[3072,512]{1,0:T(8,128)(2,1)} %get-tuple-element.67) | copy-start | bytes 9437188
  384.8 11.4 %copy-start.31 = (bf16[1024,512]{1,0:T(8,128)(2,1)S(1)}, bf16[1024,512]{1,0:T(8,128)(2,1)}, u32[]{:S(2)}) copy-start(bf16[1024,512]{1,0:T(8,128)(2,1)} %get-tuple-element.65) | copy-start | bytes 3145732
  386.4 2.5 collective-permute-start.17
  388.3 21.9 %collective-permute-start.15 = (bf16[3088,128]{1,0:T(8,128)(2,1)S(1)}, bf16[3088,128]{1,0:T(8,128)(2,1)S(1)}, u32[]{:S(2)}, u32[]{:S(2)}) collective-permute-start(bf16[3088,128]{1,0:T(8,128)(2,1)S(1)} %fusion.36), channel_id=1, source_target_pairs={{0,4},{2,6},{4,0},{6,2},{1,5},{3,7},{5,1},{7,3},{8,12},{10,14},{12... | collective-permute-start | bytes 2371592 | tf_op jit(solution)/shard_map/ppermute | solution.py:1224
  388.9 20.5 %collective-permute-start.18 = (f32[48,128]{1,0:T(8,128)S(1)}, f32[48,128]{1,0:T(8,128)S(1)}, u32[]{:S(2)}, u32[]{:S(2)}) collective-permute-start(f32[48,128]{1,0:T(8,128)S(1)} %fusion.48), channel_id=1, source_target_pairs={{0,4},{2,6},{4,0},{6,2},{1,5},{3,7},{5,1},{7,3},{8,12},{10,14},{12... | collective-permute-start | bytes 73736 | tf_op jit(solution)/shard_map/ppermute | solution.py:1224
  392.7 57.1 %collective-permute-start.9 = (bf16[3088,128]{1,0:T(8,128)(2,1)}, bf16[3088,128]{1,0:T(8,128)(2,1)}, u32[]{:S(2)}, u32[]{:S(2)}) collective-permute-start(bf16[3088,128]{1,0:T(8,128)(2,1)} %fusion.33), channel_id=1, source_target_pairs={{0,4},{2,6},{4,0},{6,2},{1,5},{3,7},{5,1},{7,3},{8,12},{10,14},{12... | collective-permute-start | bytes 2371592 | tf_op jit(solution)/shard_map/ppermute | solution.py:1224
  393.2 1.4 copy-start.7
  394.7 47.8 %collective-permute-start.11 = (bf16[3088,128]{1,0:T(8,128)(2,1)}, bf16[3088,128]{1,0:T(8,128)(2,1)}, u32[]{:S(2)}, u32[]{:S(2)}) collective-permute-start(bf16[3088,128]{1,0:T(8,128)(2,1)} %fusion.34), channel_id=1, source_target_pairs={{0,4},{2,6},{4,0},{6,2},{1,5},{3,7},{5,1},{7,3},{8,12},{10,14},{12... | collective-permute-start | bytes 2371592 | tf_op jit(solution)/shard_map/ppermute | solution.py:1224
  399.7 2.0 copy-start.8
  409.4 71.5 %collective-permute-start.7 = (bf16[512,1024]{1,0:T(8,128)(2,1)S(1)}, bf16[512,1024]{1,0:T(8,128)(2,1)}, u32[]{:S(2)}, u32[]{:S(2)}) collective-permute-start(bf16[512,1024]{1,0:T(8,128)(2,1)S(1)} %slice.191), channel_id=1, source_target_pairs={{0,1},{1,0},{2,3},{3,2},{4,5},{5,4},{6,7},{7,6},{8,9},{9,8},{10,11... | collective-permute-start | bytes 3145736 | tf_op jit(solution)/shard_map/ppermute | solution.py:1103
  410.2 0.9 copy-start.18
  449.9 7.5 %copy-start.19 = (bf16[3088,128]{1,0:T(8,128)(2,1)S(1)}, bf16[3088,128]{1,0:T(8,128)(2,1)}, u32[]{:S(2)}) copy-start(bf16[3088,128]{1,0:T(8,128)(2,1)} %get-tuple-element.97) | copy-start | bytes 2371588
  449.9 7.5 %copy-start.20 = (bf16[3088,128]{1,0:T(8,128)(2,1)S(1)}, bf16[3088,128]{1,0:T(8,128)(2,1)}, u32[]{:S(2)}) copy-start(bf16[3088,128]{1,0:T(8,128)(2,1)} %get-tuple-element.94) | copy-start | bytes 2371588
  449.9 7.5 %copy-start.21 = (bf16[3088,128]{1,0:T(8,128)(2,1)S(1)}, bf16[3088,128]{1,0:T(8,128)(2,1)}, u32[]{:S(2)}) copy-start(bf16[3088,128]{1,0:T(8,128)(2,1)} %get-tuple-element.95) | copy-start | bytes 2371588
  457.4 23.5 %copy-start.9 = (f32[1024,1024]{1,0:T(8,128)S(1)}, f32[1024,1024]{1,0:T(8,128)}, u32[]{:S(2)}) copy-start(f32[1024,1024]{1,0:T(8,128)} %copy-done.8) | copy-start | bytes 12582916
  460.0 42.0 %collective-permute-start.19 = (bf16[3088,128]{1,0:T(8,128)(2,1)S(1)}, bf16[3088,128]{1,0:T(8,128)(2,1)S(1)}, u32[]{:S(2)}, u32[]{:S(2)}) collective-permute-start(bf16[3088,128]{1,0:T(8,128)(2,1)S(1)} %get-tuple-element.122), channel_id=1, source_target_pairs={{0,8},{8,0},{16,24},{24,16},{1,9},{9,1},{17,25},{25,17},{2,10},{10... | collective-permute-start | bytes 2371592 | tf_op jit(solution)/shard_map/ppermute | solution.py:1224
  469.7 62.6 %collective-permute-start.20 = (bf16[3088,128]{1,0:T(8,128)(2,1)S(1)}, bf16[3088,128]{1,0:T(8,128)(2,1)S(1)}, u32[]{:S(2)}, u32[]{:S(2)}) collective-permute-start(bf16[3088,128]{1,0:T(8,128)(2,1)S(1)} %get-tuple-element.121), channel_id=1, source_target_pairs={{0,16},{8,24},{16,0},{24,8},{1,17},{9,25},{17,1},{25,9},{2,18},{10... | collective-permute-start | bytes 2371592 | tf_op jit(solution)/shard_map/ppermute | solution.py:1224
  480.3 68.2 %collective-permute-start.21 = (bf16[3088,128]{1,0:T(8,128)(2,1)S(1)}, bf16[3088,128]{1,0:T(8,128)(2,1)S(1)}, u32[]{:S(2)}, u32[]{:S(2)}) collective-permute-start(bf16[3088,128]{1,0:T(8,128)(2,1)S(1)} %get-tuple-element.120), channel_id=1, source_target_pairs={{0,24},{8,16},{16,8},{24,0},{1,25},{9,17},{17,9},{25,1},{2,26},{10... | collective-permute-start | bytes 2371592 | tf_op jit(solution)/shard_map/ppermute | solution.py:1224
  502.0 46.5 %copy-start.22 = (bf16[3088,128]{1,0:T(8,128)(2,1)}, bf16[3088,128]{1,0:T(8,128)(2,1)S(1)}, u32[]{:S(2)}) copy-start(bf16[3088,128]{1,0:T(8,128)(2,1)S(1)} %collective-permute-done.19.d1) | copy-start | bytes 2371588
  532.3 16.2 %copy-start.23 = (bf16[3088,128]{1,0:T(8,128)(2,1)}, bf16[3088,128]{1,0:T(8,128)(2,1)S(1)}, u32[]{:S(2)}) copy-start(bf16[3088,128]{1,0:T(8,128)(2,1)S(1)} %collective-permute-done.20.d2) | copy-start | bytes 2371588
  548.5 0.9 copy-start.24
